TPU v7x, 256 devices: a whole 4x4x8 slice. The times are simulated.
256 devices in a mesh: section: 8 (over y, core), tile: 32 (over x, z).
Axes of the slice: x: 4, y: 4, z: 8, core: 2. Of those that a mesh axis runs over, the one named last changes fastest.
Arguments:
- latent: bfloat16 [1, 18432, 1536], P(None, 'tile'), may hold values from -6 to 6
- w_qkv: bfloat16 [8, 1536, 4608], P('section', 'tile'), may hold values from -0.15625 to 0.15625
- mod_shift: float32 [8, 1536], P('section'), may hold values from -3 to 3
- mod_scale: float32 [8, 1536], P('section'), may hold values from 0.25 to 1.75
- attn_gate: float32 [8, 1536], P('section'), may hold values from 0.5 to 1.5
- qk_gain: float32 [8, 128], P('section'), may hold values from 0.8 to 2
- slot_tile: int32 [96], replicated, may hold values from 0 to 95, as said below
- window_tiles: int32 [96, 27], replicated, may hold values from -1 to 95, as said below
Outputs:
- layer_states: bfloat16 [8, 1, 18432, 1536], P('section', None, 'tile')
Inputs may be any that keep to these rules, and one draw needn't show every extreme that they name: `slot_tile`: A permutation of the 96 tile ids. `window_tiles`: row t lists the tiles of the 3 x 3 x 3 tile window around tile t in the latent's frame, height and width (t itself included), -1 where the window leaves the latent; no id twice in a row. Every listed tile is stored in a slot of the same tile device as t's slot or of one of the two tile devices beside it, cyclically (device i holds slots i * 3 to (i + 1) * 3 - 1).
All inputs are finite; a program needn't handle non-finite values.
Results may differ from a plain program's by a relative error of at most 0.01.
Values may be sent and summed in bfloat16 or wider, within the bound.
A program may use at most 128 MiB of HBM per device.

v0:
```python
import jax
import jax.numpy as jnp
from jax import lax
from jax.sharding import PartitionSpec as P

TILE = 192
GRID_H = 1
GRID_W = 3


EPS = 1e-06


def extended(block, sides, width):
    for axis, dim in sides:
        count = lax.axis_size(axis)
        forward = [(i, i + 1) for i in range(count - 1)]
        forward.append((count - 1, 0))
        backward = [(target, source) for source, target in forward]
        low = lax.ppermute(
            lax.slice_in_dim(block, block.shape[dim] - width, None, axis=dim), axis, forward
        )
        high = lax.ppermute(lax.slice_in_dim(block, 0, width, axis=dim), axis, backward)
        block = jnp.concatenate([low, block, high], axis=dim)
    return block


def shifted(block, axis, distance):
    devices = range(lax.axis_size(axis))
    route = [(i - distance, i) for i in devices if i - distance in devices]
    return lax.ppermute(block, axis, route)


def modulate(hidden, shifts, scales):
    numbers = hidden.astype(jnp.float32)
    average = jnp.mean(numbers, axis=-1, keepdims=True)
    centred = numbers - average
    spread = jnp.mean(centred * centred, axis=-1, keepdims=True)
    normed = centred * lax.rsqrt(spread + EPS)
    return (normed * scales + shifts).astype(jnp.bfloat16)


def head_norm(numbers, gain_values):
    square_mean = jnp.mean(numbers * numbers, axis=-1, keepdims=True)
    return (numbers * lax.rsqrt(square_mean + EPS) * gain_values).astype(jnp.bfloat16)


def window_mask(slot_tile, window_tiles, per_device):
    tile_count = lax.axis_size("tile")
    tile_place = lax.axis_index("tile")
    own_ids = lax.dynamic_slice_in_dim(slot_tile, tile_place * per_device, per_device)
    blocks = []
    for offset in (-1, 0, 1):
        neighbour = (tile_place + offset + tile_count) % tile_count
        blocks.append(lax.dynamic_slice_in_dim(slot_tile, neighbour * per_device, per_device))
    key_ids = jnp.concatenate(blocks)
    picked = own_ids[:, None] == jnp.arange(window_tiles.shape[0], dtype=jnp.int32)[None, :]
    listed = jnp.sum(jnp.where(picked[:, :, None], window_tiles[None], 0), axis=1)
    return jnp.any(listed[:, :, None] == key_ids[None, None, :], axis=1)


def prepare(hidden, whole_weights, shifts, scales, gain_values):
    groups, tokens, model_width = hidden.shape
    head_dim = gain_values.shape[-1]
    head_count = model_width // head_dim
    modded = modulate(hidden, shifts, scales)
    projected = jnp.einsum("gtw,wo->gto", modded, whole_weights, preferred_element_type=jnp.float32)
    shaped = projected.reshape(groups, tokens, 3, head_count, head_dim)
    queries = head_norm(shaped[:, :, 0], gain_values)
    key_heads = head_norm(shaped[:, :, 1], gain_values)
    values = shaped[:, :, 2].astype(jnp.bfloat16)
    key_value = jnp.concatenate((key_heads, values), axis=2).reshape(
        groups, tokens, 2 * model_width
    )
    return (queries, key_value)


def attend(queries, widened, allowed, tile_len):
    groups, tokens, head_count, head_dim = queries.shape
    model_width = head_count * head_dim
    widened = widened.reshape(groups, 3 * tokens, 2, head_count, head_dim)
    token_mask = jnp.repeat(jnp.repeat(allowed, tile_len, axis=0), tile_len, axis=1)
    query_heads = jnp.moveaxis(queries, 2, 0)
    far_keys = jnp.moveaxis(widened[:, :, 0], 2, 0)
    far_values = jnp.moveaxis(widened[:, :, 1], 2, 0)

    def one_head(operands):
        head_queries, head_keys, head_values = operands
        scores = jnp.einsum(
            "gqd,gkd->gqk", head_queries, head_keys, preferred_element_type=jnp.float32
        )
        scores = scores * head_dim ** (-0.5)
        scores = jnp.where(token_mask[None], scores, -jnp.inf)
        row_max = jnp.max(scores, axis=-1, keepdims=True)
        powers = jnp.exp(scores - row_max)
        row_sum = jnp.sum(powers, axis=-1, keepdims=True)
        probs = (powers / row_sum).astype(jnp.bfloat16)
        return jnp.einsum("gqk,gkd->gqd", probs, head_values, preferred_element_type=jnp.float32)

    attended = lax.map(one_head, (query_heads, far_keys, far_values))
    attended = jnp.moveaxis(attended, 0, 2)
    return attended.reshape(groups, tokens, model_width)


def run_layer(
    hidden, active, whole_weights, shifts, scales, gate_values, gain_values, allowed, tile_len
):
    groups, tokens, model_width = hidden.shape
    head_dim = gain_values.shape[-1]
    head_count = model_width // head_dim

    def skip_prepare(block_in):
        return (
            jnp.zeros((groups, tokens, head_count, head_dim), jnp.bfloat16),
            jnp.zeros((groups, tokens, 2 * model_width), jnp.bfloat16),
        )

    queries, key_value = lax.cond(
        active,
        lambda block_in: prepare(block_in, whole_weights, shifts, scales, gain_values),
        skip_prepare,
        hidden,
    )
    widened = extended(key_value, (("tile", 1),), tokens)
    attended = lax.cond(
        active,
        lambda operands: attend(operands[0], operands[1], allowed, tile_len),
        lambda operands: jnp.zeros((groups, tokens, model_width), jnp.float32),
        (queries, widened),
    )
    updated = (hidden.astype(jnp.float32) + gate_values * attended).astype(jnp.bfloat16)
    return jnp.where(active, updated, hidden)


def hand_on(block_out):
    return shifted(block_out, "section", 1)


def on_device(latent, w_qkv, mod_shift, mod_scale, attn_gate, qk_gain, slot_tile, window_tiles):
    sections = lax.axis_size("section")
    section_place = lax.axis_index("section")
    micro_count, tokens, model_width = latent.shape
    per_device = GRID_H * GRID_W
    tile_len = TILE
    allowed = window_mask(slot_tile, window_tiles, per_device)
    shifts = mod_shift[0]
    scales = mod_scale[0]
    gate_values = attn_gate[0]
    gain_values = qk_gain[0]
    weight_part = w_qkv[0]
    whole_weights = lax.all_gather(weight_part, "tile", axis=0, tiled=True)

    def layer_step(layer_index, loop_state):
        incoming, states = loop_state
        current = jnp.where(section_place == 0, latent, incoming)
        active = layer_index == section_place
        result = run_layer(
            current,
            active,
            whole_weights,
            shifts,
            scales,
            gate_values,
            gain_values,
            allowed,
            tile_len,
        )
        states = jnp.where(active, result, states)
        return (hand_on(result), states)

    initial = (
        jnp.zeros((micro_count, tokens, model_width), jnp.bfloat16),
        jnp.zeros((micro_count, tokens, model_width), jnp.bfloat16),
    )
    final_state = lax.fori_loop(0, sections, layer_step, initial)
    states = final_state[1]
    return states[None]


def solution(mesh):
    return jax.shard_map(
        on_device,
        mesh=mesh,
        in_specs=(
            P(None, "tile", None),
            P("section", "tile", None),
            P("section", None),
            P("section", None),
            P("section", None),
            P("section", None),
            P(),
            P(),
        ),
        out_specs=P("section", None, "tile", None),
        check_vma=False,
    )
```

profile of v0, /device:TPU:25, one launch (start us, length us, event | category | flops | bytes accessed | tf_op | source)
XLA Modules:
  0.0 2120.9 jit_solution(9977201617806583457)
XLA Ops:
  10.2 129.3 %all-gather.3.cloned.1.call-done = bf16[1,1536,4608]{2,1,0:T(8,128)(2,1)} async-done(((bf16[1,48,4608]{2,1,0:T(8,128)(2,1)}), bf16[1,1536,4608]{2,1,0:T(8,128)(2,1)}) %all-gather.3.cloned.1.call-update) | async-done | bytes 14155792 | tf_op jit(solution)/shard_map/all_gather | solution.py:151
  139.4 18.7 copy.46
  158.2 1955.8 %while.28 = (s32[]{:T(128)}, bf16[1,576,1536]{2,1,0:T(8,128)(2,1)S(1)}, bf16[1,576,1536]{2,1,0:T(8,128)(2,1)}, s32[]{:T(128)}, pred[]{:T(512)}, /*index=5*/bf16[...) while((s32[]{:T(128)}, ...), condition=%wide.region_15.16_spmd.clone, body=%wide.region_2.15_spmd.clone.sunk | while | flops 8731472896 | bytes 226495536 | solution.py:175
  163.1 75.2 %collective-permute-done = bf16[1,576,3072]{2,1,0:T(8,128)(2,1)} collective-permute-done((bf16[1,576,3072]{2,1,0:T(8,128)(2,1)}, bf16[1,576,3072]{2,1,0:T(8,128)(2,1)}, u32[]{:S(2)}, u32[]{:S(2)}) %collective-permute-start) | collective-permute-done | bytes 3538976 | tf_op jit(solution)/shard_map/while/body/eval_jaxpr/ppermute | solution.py:23
  242.8 9.4 pad_maximum_fusion.2
  271.5 57.5 %collective-permute-done = bf16[1,576,3072]{2,1,0:T(8,128)(2,1)} collective-permute-done((bf16[1,576,3072]{2,1,0:T(8,128)(2,1)}, bf16[1,576,3072]{2,1,0:T(8,128)(2,1)}, u32[]{:S(2)}, u32[]{:S(2)}) %collective-permute-start) | collective-permute-done | bytes 3538976 | tf_op jit(solution)/shard_map/while/body/eval_jaxpr/ppermute | solution.py:23
  332.2 9.4 pad_maximum_fusion.2
  350.4 23.9 %collective-permute-done.2 = bf16[1,576,1536]{2,1,0:T(8,128)(2,1)S(1)} collective-permute-done((bf16[1,576,1536]{2,1,0:T(8,128)(2,1)}, bf16[1,576,1536]{2,1,0:T(8,128)(2,1)S(1)}, u32[]{:S(2)}, u32[]{:S(2)}) %collective-permute-start.2) | collective-permute-done | bytes 1769504 | tf_op jit(solution)/shard_map/while/body/eval_jaxpr/ppermute | solution.py:31
  379.1 43.8 %collective-permute-done = bf16[1,576,3072]{2,1,0:T(8,128)(2,1)} collective-permute-done((bf16[1,576,3072]{2,1,0:T(8,128)(2,1)}, bf16[1,576,3072]{2,1,0:T(8,128)(2,1)}, u32[]{:S(2)}, u32[]{:S(2)}) %collective-permute-start) | collective-permute-done | bytes 3538976 | tf_op jit(solution)/shard_map/while/body/eval_jaxpr/ppermute | solution.py:23
  444.2 37.7 %collective-permute-done.2 = bf16[1,576,1536]{2,1,0:T(8,128)(2,1)S(1)} collective-permute-done((bf16[1,576,1536]{2,1,0:T(8,128)(2,1)}, bf16[1,576,1536]{2,1,0:T(8,128)(2,1)S(1)}, u32[]{:S(2)}, u32[]{:S(2)}) %collective-permute-start.2) | collective-permute-done | bytes 1769504 | tf_op jit(solution)/shard_map/while/body/eval_jaxpr/ppermute | solution.py:31
  486.8 38.6 %collective-permute-done = bf16[1,576,3072]{2,1,0:T(8,128)(2,1)} collective-permute-done((bf16[1,576,3072]{2,1,0:T(8,128)(2,1)}, bf16[1,576,3072]{2,1,0:T(8,128)(2,1)}, u32[]{:S(2)}, u32[]{:S(2)}) %collective-permute-start) | collective-permute-done | bytes 3538976 | tf_op jit(solution)/shard_map/while/body/eval_jaxpr/ppermute | solution.py:23
  546.9 48.4 %collective-permute-done.2 = bf16[1,576,1536]{2,1,0:T(8,128)(2,1)S(1)} collective-permute-done((bf16[1,576,1536]{2,1,0:T(8,128)(2,1)}, bf16[1,576,1536]{2,1,0:T(8,128)(2,1)S(1)}, u32[]{:S(2)}, u32[]{:S(2)}) %collective-permute-start.2) | collective-permute-done | bytes 1769504 | tf_op jit(solution)/shard_map/while/body/eval_jaxpr/ppermute | solution.py:31
  600.2 38.8 %collective-permute-done = bf16[1,576,3072]{2,1,0:T(8,128)(2,1)} collective-permute-done((bf16[1,576,3072]{2,1,0:T(8,128)(2,1)}, bf16[1,576,3072]{2,1,0:T(8,128)(2,1)}, u32[]{:S(2)}, u32[]{:S(2)}) %collective-permute-start) | collective-permute-done | bytes 3538976 | tf_op jit(solution)/shard_map/while/body/eval_jaxpr/ppermute | solution.py:23
  660.4 49.8 %collective-permute-done.2 = bf16[1,576,1536]{2,1,0:T(8,128)(2,1)S(1)} collective-permute-done((bf16[1,576,1536]{2,1,0:T(8,128)(2,1)}, bf16[1,576,1536]{2,1,0:T(8,128)(2,1)S(1)}, u32[]{:S(2)}, u32[]{:S(2)}) %collective-permute-start.2) | collective-permute-done | bytes 1769504 | tf_op jit(solution)/shard_map/while/body/eval_jaxpr/ppermute | solution.py:31
  715.1 57.5 %collective-permute-done = bf16[1,576,3072]{2,1,0:T(8,128)(2,1)} collective-permute-done((bf16[1,576,3072]{2,1,0:T(8,128)(2,1)}, bf16[1,576,3072]{2,1,0:T(8,128)(2,1)}, u32[]{:S(2)}, u32[]{:S(2)}) %collective-permute-start) | collective-permute-done | bytes 3538976 | tf_op jit(solution)/shard_map/while/body/eval_jaxpr/ppermute | solution.py:23
  794.1 23.7 %collective-permute-done.2 = bf16[1,576,1536]{2,1,0:T(8,128)(2,1)S(1)} collective-permute-done((bf16[1,576,1536]{2,1,0:T(8,128)(2,1)}, bf16[1,576,1536]{2,1,0:T(8,128)(2,1)S(1)}, u32[]{:S(2)}, u32[]{:S(2)}) %collective-permute-start.2) | collective-permute-done | bytes 1769504 | tf_op jit(solution)/shard_map/while/body/eval_jaxpr/ppermute | solution.py:31
  822.7 38.6 %collective-permute-done = bf16[1,576,3072]{2,1,0:T(8,128)(2,1)} collective-permute-done((bf16[1,576,3072]{2,1,0:T(8,128)(2,1)}, bf16[1,576,3072]{2,1,0:T(8,128)(2,1)}, u32[]{:S(2)}, u32[]{:S(2)}) %collective-permute-start) | collective-permute-done | bytes 3538976 | tf_op jit(solution)/shard_map/while/body/eval_jaxpr/ppermute | solution.py:23
  882.8 976.8 %collective-permute-done.2 = bf16[1,576,1536]{2,1,0:T(8,128)(2,1)S(1)} collective-permute-done((bf16[1,576,1536]{2,1,0:T(8,128)(2,1)}, bf16[1,576,1536]{2,1,0:T(8,128)(2,1)S(1)}, u32[]{:S(2)}, u32[]{:S(2)}) %collective-permute-start.2) | collective-permute-done | bytes 1769504 | tf_op jit(solution)/shard_map/while/body/eval_jaxpr/ppermute | solution.py:31
  1859.9 19.5 conditional.6
  1860.9 11.3 convolution_bitcast_fusion
  1881.5 74.4 %collective-permute-done = bf16[1,576,3072]{2,1,0:T(8,128)(2,1)} collective-permute-done((bf16[1,576,3072]{2,1,0:T(8,128)(2,1)}, bf16[1,576,3072]{2,1,0:T(8,128)(2,1)}, u32[]{:S(2)}, u32[]{:S(2)}) %collective-permute-start) | collective-permute-done | bytes 3538976 | tf_op jit(solution)/shard_map/while/body/eval_jaxpr/ppermute | solution.py:23
  1968.5 134.5 %conditional.7 = (f32[1,576,1536]{2,1,0:T(8,128)}) conditional(s32[]{:T(128)} %convert_element_type.112, () %tuple.98, (bf16[1,576,12,128]{3,1,2,0:T(8,128)(2,1)S(1)}, bf16[1,1728,3072]{2,1,0:T(8,128)(2,1)}, pred[3,9]{0,1:T(8,128)(4,1)S(1)}) %tuple.123), branch_computations={%region_9.9_spmd, %region_10.14_spmd} | conditional | flops 517569408 | bytes 95180464 | solution.py:125
  1968.5 14.0 copy.44
  2009.6 82.7 %while.27 = (s32[]{:T(128)}, f32[12,1,576,128]{3,2,1,0:T(8,128)}, bf16[12,1,576,128]{3,2,1,0:T(8,128)(2,1)S(1)}, bf16[12,1,1728,128]{3,2,1,0:T(8,128)(2,1)}, bf1...) while((s32[]{:T(128)}, f32[12,1,576,128]{3,2,1,0:T(8,128)}, ...), condition=%wide.region_14.13_spmd.clone, body=%wide.region_11.12_spmd.clone.sunk | while | flops 517569408 | bytes 17308044 | solution.py:100
  (243 shorter events, 363.1 us)
Async XLA Ops:
  6.5 132.9 %all-gather.3.cloned.1.call-start = ((), (), s32[]{:S(2)}) async-start(), calls=%async_computation | async-start | bytes 14598144 | tf_op jit(solution)/shard_map/all_gather | solution.py:151
  161.0 77.4 %collective-permute-start = (bf16[1,576,3072]{2,1,0:T(8,128)(2,1)}, bf16[1,576,3072]{2,1,0:T(8,128)(2,1)}, u32[]{:S(2)}, u32[]{:S(2)}) collective-permute-start(bf16[1,576,3072]{2,1,0:T(8,128)(2,1)} %get-tuple-element.603), channel_id=1, source_target_pairs={{1,0},{2,1},{3,2},{4,3},{5,4},{6,5},{7,6},{8,7},{9,8},{10,9},{11,1... | collective-permute-start | bytes 10616840 | tf_op jit(solution)/shard_map/while/body/eval_jaxpr/ppermute | solution.py:23
  162.4 80.3 %collective-permute-start.1 = (bf16[1,576,3072]{2,1,0:T(8,128)(2,1)}, bf16[1,576,3072]{2,1,0:T(8,128)(2,1)}, u32[]{:S(2)}, u32[]{:S(2)}) collective-permute-start(bf16[1,576,3072]{2,1,0:T(8,128)(2,1)} %get-tuple-element.603), channel_id=1, source_target_pairs={{0,1},{1,2},{2,3},{3,4},{4,5},{5,6},{6,7},{7,8},{8,9},{9,10},{10,1... | collective-permute-start | bytes 10616840 | tf_op jit(solution)/shard_map/while/body/eval_jaxpr/ppermute | solution.py:20
  259.1 7.5 collective-permute-start.2
  269.4 59.7 %collective-permute-start = (bf16[1,576,3072]{2,1,0:T(8,128)(2,1)}, bf16[1,576,3072]{2,1,0:T(8,128)(2,1)}, u32[]{:S(2)}, u32[]{:S(2)}) collective-permute-start(bf16[1,576,3072]{2,1,0:T(8,128)(2,1)} %get-tuple-element.603), channel_id=1, source_target_pairs={{1,0},{2,1},{3,2},{4,3},{5,4},{6,5},{7,6},{8,7},{9,8},{10,9},{11,1... | collective-permute-start | bytes 10616840 | tf_op jit(solution)/shard_map/while/body/eval_jaxpr/ppermute | solution.py:23
  269.4 62.8 %collective-permute-start.1 = (bf16[1,576,3072]{2,1,0:T(8,128)(2,1)}, bf16[1,576,3072]{2,1,0:T(8,128)(2,1)}, u32[]{:S(2)}, u32[]{:S(2)}) collective-permute-start(bf16[1,576,3072]{2,1,0:T(8,128)(2,1)} %get-tuple-element.603), channel_id=1, source_target_pairs={{0,1},{1,2},{2,3},{3,4},{4,5},{5,6},{6,7},{7,8},{8,9},{9,10},{10,1... | collective-permute-start | bytes 10616840 | tf_op jit(solution)/shard_map/while/body/eval_jaxpr/ppermute | solution.py:20
  349.1 25.2 %collective-permute-start.2 = (bf16[1,576,1536]{2,1,0:T(8,128)(2,1)}, bf16[1,576,1536]{2,1,0:T(8,128)(2,1)S(1)}, u32[]{:S(2)}, u32[]{:S(2)}) collective-permute-start(bf16[1,576,1536]{2,1,0:T(8,128)(2,1)} %get-tuple-element.605), channel_id=1, source_target_pairs={{0,32},{32,64},{64,96},{96,128},{128,160},{160,192},{192,224},{1,3... | collective-permute-start | bytes 5308424 | tf_op jit(solution)/shard_map/while/body/eval_jaxpr/ppermute | solution.py:31
  377.0 46.0 %collective-permute-start = (bf16[1,576,3072]{2,1,0:T(8,128)(2,1)}, bf16[1,576,3072]{2,1,0:T(8,128)(2,1)}, u32[]{:S(2)}, u32[]{:S(2)}) collective-permute-start(bf16[1,576,3072]{2,1,0:T(8,128)(2,1)} %get-tuple-element.603), channel_id=1, source_target_pairs={{1,0},{2,1},{3,2},{4,3},{5,4},{6,5},{7,6},{8,7},{9,8},{10,9},{11,1... | collective-permute-start | bytes 10616840 | tf_op jit(solution)/shard_map/while/body/eval_jaxpr/ppermute | solution.py:23
  377.1 49.0 %collective-permute-start.1 = (bf16[1,576,3072]{2,1,0:T(8,128)(2,1)}, bf16[1,576,3072]{2,1,0:T(8,128)(2,1)}, u32[]{:S(2)}, u32[]{:S(2)}) collective-permute-start(bf16[1,576,3072]{2,1,0:T(8,128)(2,1)} %get-tuple-element.603), channel_id=1, source_target_pairs={{0,1},{1,2},{2,3},{3,4},{4,5},{5,6},{6,7},{7,8},{8,9},{9,10},{10,1... | collective-permute-start | bytes 10616840 | tf_op jit(solution)/shard_map/while/body/eval_jaxpr/ppermute | solution.py:20
  442.9 39.0 %collective-permute-start.2 = (bf16[1,576,1536]{2,1,0:T(8,128)(2,1)}, bf16[1,576,1536]{2,1,0:T(8,128)(2,1)S(1)}, u32[]{:S(2)}, u32[]{:S(2)}) collective-permute-start(bf16[1,576,1536]{2,1,0:T(8,128)(2,1)} %get-tuple-element.605), channel_id=1, source_target_pairs={{0,32},{32,64},{64,96},{96,128},{128,160},{160,192},{192,224},{1,3... | collective-permute-start | bytes 5308424 | tf_op jit(solution)/shard_map/while/body/eval_jaxpr/ppermute | solution.py:31
  484.6 40.7 %collective-permute-start = (bf16[1,576,3072]{2,1,0:T(8,128)(2,1)}, bf16[1,576,3072]{2,1,0:T(8,128)(2,1)}, u32[]{:S(2)}, u32[]{:S(2)}) collective-permute-start(bf16[1,576,3072]{2,1,0:T(8,128)(2,1)} %get-tuple-element.603), channel_id=1, source_target_pairs={{1,0},{2,1},{3,2},{4,3},{5,4},{6,5},{7,6},{8,7},{9,8},{10,9},{11,1... | collective-permute-start | bytes 10616840 | tf_op jit(solution)/shard_map/while/body/eval_jaxpr/ppermute | solution.py:23
  484.7 44.0 %collective-permute-start.1 = (bf16[1,576,3072]{2,1,0:T(8,128)(2,1)}, bf16[1,576,3072]{2,1,0:T(8,128)(2,1)}, u32[]{:S(2)}, u32[]{:S(2)}) collective-permute-start(bf16[1,576,3072]{2,1,0:T(8,128)(2,1)} %get-tuple-element.603), channel_id=1, source_target_pairs={{0,1},{1,2},{2,3},{3,4},{4,5},{5,6},{6,7},{7,8},{8,9},{9,10},{10,1... | collective-permute-start | bytes 10616840 | tf_op jit(solution)/shard_map/while/body/eval_jaxpr/ppermute | solution.py:20
  545.6 49.7 %collective-permute-start.2 = (bf16[1,576,1536]{2,1,0:T(8,128)(2,1)}, bf16[1,576,1536]{2,1,0:T(8,128)(2,1)S(1)}, u32[]{:S(2)}, u32[]{:S(2)}) collective-permute-start(bf16[1,576,1536]{2,1,0:T(8,128)(2,1)} %get-tuple-element.605), channel_id=1, source_target_pairs={{0,32},{32,64},{64,96},{96,128},{128,160},{160,192},{192,224},{1,3... | collective-permute-start | bytes 5308424 | tf_op jit(solution)/shard_map/while/body/eval_jaxpr/ppermute | solution.py:31
  598.1 40.9 %collective-permute-start = (bf16[1,576,3072]{2,1,0:T(8,128)(2,1)}, bf16[1,576,3072]{2,1,0:T(8,128)(2,1)}, u32[]{:S(2)}, u32[]{:S(2)}) collective-permute-start(bf16[1,576,3072]{2,1,0:T(8,128)(2,1)} %get-tuple-element.603), channel_id=1, source_target_pairs={{1,0},{2,1},{3,2},{4,3},{5,4},{6,5},{7,6},{8,7},{9,8},{10,9},{11,1... | collective-permute-start | bytes 10616840 | tf_op jit(solution)/shard_map/while/body/eval_jaxpr/ppermute | solution.py:23
  598.1 44.0 %collective-permute-start.1 = (bf16[1,576,3072]{2,1,0:T(8,128)(2,1)}, bf16[1,576,3072]{2,1,0:T(8,128)(2,1)}, u32[]{:S(2)}, u32[]{:S(2)}) collective-permute-start(bf16[1,576,3072]{2,1,0:T(8,128)(2,1)} %get-tuple-element.603), channel_id=1, source_target_pairs={{0,1},{1,2},{2,3},{3,4},{4,5},{5,6},{6,7},{7,8},{8,9},{9,10},{10,1... | collective-permute-start | bytes 10616840 | tf_op jit(solution)/shard_map/while/body/eval_jaxpr/ppermute | solution.py:20
  659.1 51.1 %collective-permute-start.2 = (bf16[1,576,1536]{2,1,0:T(8,128)(2,1)}, bf16[1,576,1536]{2,1,0:T(8,128)(2,1)S(1)}, u32[]{:S(2)}, u32[]{:S(2)}) collective-permute-start(bf16[1,576,1536]{2,1,0:T(8,128)(2,1)} %get-tuple-element.605), channel_id=1, source_target_pairs={{0,32},{32,64},{64,96},{96,128},{128,160},{160,192},{192,224},{1,3... | collective-permute-start | bytes 5308424 | tf_op jit(solution)/shard_map/while/body/eval_jaxpr/ppermute | solution.py:31
  712.9 59.7 %collective-permute-start = (bf16[1,576,3072]{2,1,0:T(8,128)(2,1)}, bf16[1,576,3072]{2,1,0:T(8,128)(2,1)}, u32[]{:S(2)}, u32[]{:S(2)}) collective-permute-start(bf16[1,576,3072]{2,1,0:T(8,128)(2,1)} %get-tuple-element.603), channel_id=1, source_target_pairs={{1,0},{2,1},{3,2},{4,3},{5,4},{6,5},{7,6},{8,7},{9,8},{10,9},{11,1... | collective-permute-start | bytes 10616840 | tf_op jit(solution)/shard_map/while/body/eval_jaxpr/ppermute | solution.py:23
  713.0 63.0 %collective-permute-start.1 = (bf16[1,576,3072]{2,1,0:T(8,128)(2,1)}, bf16[1,576,3072]{2,1,0:T(8,128)(2,1)}, u32[]{:S(2)}, u32[]{:S(2)}) collective-permute-start(bf16[1,576,3072]{2,1,0:T(8,128)(2,1)} %get-tuple-element.603), channel_id=1, source_target_pairs={{0,1},{1,2},{2,3},{3,4},{4,5},{5,6},{6,7},{7,8},{8,9},{9,10},{10,1... | collective-permute-start | bytes 10616840 | tf_op jit(solution)/shard_map/while/body/eval_jaxpr/ppermute | solution.py:20
  792.9 25.0 %collective-permute-start.2 = (bf16[1,576,1536]{2,1,0:T(8,128)(2,1)}, bf16[1,576,1536]{2,1,0:T(8,128)(2,1)S(1)}, u32[]{:S(2)}, u32[]{:S(2)}) collective-permute-start(bf16[1,576,1536]{2,1,0:T(8,128)(2,1)} %get-tuple-element.605), channel_id=1, source_target_pairs={{0,32},{32,64},{64,96},{96,128},{128,160},{160,192},{192,224},{1,3... | collective-permute-start | bytes 5308424 | tf_op jit(solution)/shard_map/while/body/eval_jaxpr/ppermute | solution.py:31
  820.5 40.7 %collective-permute-start = (bf16[1,576,3072]{2,1,0:T(8,128)(2,1)}, bf16[1,576,3072]{2,1,0:T(8,128)(2,1)}, u32[]{:S(2)}, u32[]{:S(2)}) collective-permute-start(bf16[1,576,3072]{2,1,0:T(8,128)(2,1)} %get-tuple-element.603), channel_id=1, source_target_pairs={{1,0},{2,1},{3,2},{4,3},{5,4},{6,5},{7,6},{8,7},{9,8},{10,9},{11,1... | collective-permute-start | bytes 10616840 | tf_op jit(solution)/shard_map/while/body/eval_jaxpr/ppermute | solution.py:23
  820.6 44.0 %collective-permute-start.1 = (bf16[1,576,3072]{2,1,0:T(8,128)(2,1)}, bf16[1,576,3072]{2,1,0:T(8,128)(2,1)}, u32[]{:S(2)}, u32[]{:S(2)}) collective-permute-start(bf16[1,576,3072]{2,1,0:T(8,128)(2,1)} %get-tuple-element.603), channel_id=1, source_target_pairs={{0,1},{1,2},{2,3},{3,4},{4,5},{5,6},{6,7},{7,8},{8,9},{9,10},{10,1... | collective-permute-start | bytes 10616840 | tf_op jit(solution)/shard_map/while/body/eval_jaxpr/ppermute | solution.py:20
  881.5 978.1 %collective-permute-start.2 = (bf16[1,576,1536]{2,1,0:T(8,128)(2,1)}, bf16[1,576,1536]{2,1,0:T(8,128)(2,1)S(1)}, u32[]{:S(2)}, u32[]{:S(2)}) collective-permute-start(bf16[1,576,1536]{2,1,0:T(8,128)(2,1)} %get-tuple-element.605), channel_id=1, source_target_pairs={{0,32},{32,64},{64,96},{96,128},{128,160},{160,192},{192,224},{1,3... | collective-permute-start | bytes 5308424 | tf_op jit(solution)/shard_map/while/body/eval_jaxpr/ppermute | solution.py:31
  1879.4 76.5 %collective-permute-start = (bf16[1,576,3072]{2,1,0:T(8,128)(2,1)}, bf16[1,576,3072]{2,1,0:T(8,128)(2,1)}, u32[]{:S(2)}, u32[]{:S(2)}) collective-permute-start(bf16[1,576,3072]{2,1,0:T(8,128)(2,1)} %get-tuple-element.603), channel_id=1, source_target_pairs={{1,0},{2,1},{3,2},{4,3},{5,4},{6,5},{7,6},{8,7},{9,8},{10,9},{11,1... | collective-permute-start | bytes 10616840 | tf_op jit(solution)/shard_map/while/body/eval_jaxpr/ppermute | solution.py:23
  1879.4 79.7 %collective-permute-start.1 = (bf16[1,576,3072]{2,1,0:T(8,128)(2,1)}, bf16[1,576,3072]{2,1,0:T(8,128)(2,1)}, u32[]{:S(2)}, u32[]{:S(2)}) collective-permute-start(bf16[1,576,3072]{2,1,0:T(8,128)(2,1)} %get-tuple-element.603), channel_id=1, source_target_pairs={{0,1},{1,2},{2,3},{3,4},{4,5},{5,6},{6,7},{7,8},{8,9},{9,10},{10,1... | collective-permute-start | bytes 10616840 | tf_op jit(solution)/shard_map/while/body/eval_jaxpr/ppermute | solution.py:20
  (29 other events, 3019.7 us)
Sparse Core Ops, SparseCore 0:
  9.9 129.4 all-gather.2
where the time goes:
time: 2120 us
  waiting for transfers between devices  1750 us (83%)
  other arithmetic  141 us (7%)
  local copies, waits for them, and re-layouts  123 us (6%)
  matrix products  66.9 us (3%)
  starting transfers between devices  22.5 us (1%)
    ppermute x8, waiting for transfers between devices, shifted(): return lax.ppermute(block, axis, route)  1170 us
    ppermute x8, waiting for transfers between devices, extended(): lax.ppermute(lax.slice_in_dim(block, 0, width, axis=dim), axis, backward)  424 us
    all_gather x1, waiting for transfers between devices, on_device(): whole_weights = lax.all_gather(weight_part, 'tile', axis=0, tiled=True)  129 us
    concatenate x8, other arithmetic, extended(): block = jnp.concatenate([low, block, high], axis=dim)  74.9 us
    another operation x23, local copies, waits for them, and re-layouts  47 us
  transfers between devices with their start and end apart: 25, of which 25 were waited for; matrix products, arithmetic and copies ran while one was open for 0% of the time, Pallas kernels for 0%

commit v1 on v0

v1 whole, which is shorter than its diff:
```python
import functools
import math

import jax
import jax.numpy as jnp
from jax import lax
from jax.experimental import pallas as pl
from jax.experimental.pallas import tpu as pltpu
from jax.sharding import PartitionSpec as P

MESH = pl.DeviceIdType.MESH
HEAD = 128
SLOTS = 3
NY = 4
NX = 4
EPS = 1e-06
NEG = -1e30


def kernel(
    layers, nx, nz, heads, tokens, lat, wp, par, bias, out,
    hbuf, mod, wbuf, parbuf, qbuf, kvo, kvn, acc,
    loc_sem, a2a_s, a2a_r, par_s, par_r, z_s, z_r, x_s, x_r, c_s, c_r, cp_s, cp_r,
    kv_s, kv_r, g_s, g_r, o_s, o_r, o_l,
):
    width = NY * heads * HEAD
    half = tokens // 2
    chunk = half // SLOTS
    shard = wp.shape[1]
    n_tile = nx * nz
    section = lax.axis_index("section")
    t = lax.axis_index("tile")
    y, c = section // 2, section % 2
    x, z = t // nz, t % nz
    sib = (2 * y + 1 - c, t)
    t_next = (section, (t + 1) % n_tile)
    t_prev = (section, (t + n_tile - 1) % n_tile)
    z_next = (section, x * nz + (z + 1) % nz)
    z_prev = (section, x * nz + (z + nz - 1) % nz)
    x_next = (section, ((x + 1) % nx) * nz + z)
    x_prev = (section, ((x + nx - 1) % nx) * nz + z)

    def y_peer(d):
        return (2 * ((y + d) % NY) + c, t)

    def remote(src, dst, send, recv, device):
        return pltpu.make_async_remote_copy(
            src_ref=src, dst_ref=dst, send_sem=send, recv_sem=recv, device_id=device, device_id_type=MESH
        )

    partners = [y_peer(1), y_peer(2), y_peer(3), sib, t_next, t_prev]
    if nz > 1:
        partners += [z_next, z_prev]
    if nx > 1:
        partners += [x_next, x_prev]
    load_h = pltpu.make_async_copy(lat.at[0, pl.ds(pl.multiple_of(half * c, 16), half)], hbuf.at[0], loc_sem.at[0])
    load_h.start()
    own_rows = pl.ds(pl.multiple_of(shard * t, 16), shard)
    load_w = pltpu.make_async_copy(wp.at[y], wbuf.at[section, own_rows], loc_sem.at[1])
    load_w.start()
    load_p = pltpu.make_async_copy(par, parbuf.at[section], loc_sem.at[2])
    load_p.start()
    barrier = pltpu.get_barrier_semaphore()
    for device in partners:
        pl.semaphore_signal(barrier, inc=1, device_id=device, device_id_type=MESH)
    pl.semaphore_wait(barrier, len(partners))

    a2a = []
    for d in (1, 2, 3):
        a2a.append(
            remote(wp.at[(y + d) % NY], wbuf.at[section, own_rows], a2a_s.at[d - 1], a2a_r.at[d - 1], y_peer(d))
        )
        a2a.append(remote(par, parbuf.at[section], par_s.at[d - 1], par_r.at[d - 1], y_peer(d)))
    for copy in a2a:
        copy.start()
    load_w.wait()
    load_p.wait()
    for copy in a2a:
        copy.wait()

    def rows_of(xx, zz):
        return pl.ds(pl.multiple_of((xx * nz + zz) * shard, 16), shard)

    right_steps = nz // 2
    left_steps = (nz - 1) // 2

    def z_copy(layer, step, way):
        k = layer // 2
        zz = (z + nz - step) % nz if way == 0 else (z + step) % nz
        ref = wbuf.at[layer, rows_of(x, zz)]
        return remote(ref, ref, z_s.at[k, step, way], z_r.at[k, step, way], z_next if way == 0 else z_prev)

    def z_event(layer, step):
        if step > 0:
            if step - 1 < right_steps:
                z_copy(layer, step - 1, 0).wait()
            if step - 1 < left_steps:
                z_copy(layer, step - 1, 1).wait()
        if step < right_steps:
            z_copy(layer, step, 0).start()
        if step < left_steps:
            z_copy(layer, step, 1).start()

    z_events = right_steps + 1

    def x_copy(layer, step, way):
        k = layer // 2
        if step == 0:
            ref = wbuf.at[layer, pl.ds(pl.multiple_of(x * nz * shard, 16), nz * shard)]
        else:
            piece = nz * shard // 2
            xx = (x + nx - 1) % nx if way == 0 else (x + 1) % nx
            ref = wbuf.at[layer, pl.ds(pl.multiple_of(xx * nz * shard + way * piece, 16), piece)]
        return remote(ref, ref, x_s.at[k, step, way], x_r.at[k, step, way], x_next if way == 0 else x_prev)

    def x_event(layer, step):
        if nx == 1:
            return
        if step > 0:
            x_copy(layer, step - 1, 0).wait()
            x_copy(layer, step - 1, 1).wait()
        if step < 2:
            x_copy(layer, step, 0).start()
            x_copy(layer, step, 1).start()

    def core_copies(layer):
        k = layer // 2
        return (
            remote(wbuf.at[layer], wbuf.at[layer], c_s.at[k], c_r.at[k], sib),
            remote(parbuf.at[layer], parbuf.at[layer], cp_s.at[k], cp_r.at[k], sib),
        )

    @pl.when(c == 0)
    def _():
        for step in range(z_events):
            z_event(0, step)
        for step in range(3):
            x_event(0, step)
        for copy in core_copies(0):
            copy.start()

    @pl.when(c == 1)
    def _():
        for step in range(z_events):
            z_event(1, step)
        x_event(1, 0)

    load_h.wait()

    ones = jnp.ones((tokens, HEAD), jnp.bfloat16)

    def dot(a, b):
        return jnp.dot(a, b, preferred_element_type=jnp.float32)

    def head_norm(numbers, gain):
        square_mean = jnp.mean(numbers * numbers, axis=-1, keepdims=True)
        return (numbers * lax.rsqrt(square_mean + EPS) * gain).astype(jnp.bfloat16)

    def one_block(j, keys, values, allowed):
        scores = lax.dot_general(
            qbuf[j], keys, (((1,), (1,)), ((), ())), preferred_element_type=jnp.float32
        )
        scores = scores.reshape(SLOTS, chunk, tokens) + allowed
        powers = jnp.exp2(scores).astype(jnp.bfloat16).reshape(half, tokens)
        return dot(powers, jnp.concatenate([values, ones], axis=1))

    def layer_step(layer, carry):
        p = layer % 2
        q = 1 - p
        gathers_z = jnp.logical_and(c == p, layer + 2 < layers)
        gathers_x = jnp.logical_and(c != p, layer + 1 < layers)

        def at_z(step):
            @pl.when(gathers_z)
            def _():
                z_event(layer + 2, step)
                if step == z_events - 1:
                    x_event(layer + 2, 0)

        def at_x(step):
            @pl.when(gathers_x)
            def _():
                x_event(layer + 1, step)
                if step == 2:
                    for copy in core_copies(layer + 1):
                        copy.start()

        z_plan = [[] for _ in range(5)]
        for step in range(z_events):
            z_plan[step if step < z_events - 1 else 4].append(step)

        def at(place):
            for step in z_plan[place]:
                at_z(step)
            if place == 1:
                at_x(1)
            if place == 3:
                at_x(2)

        @pl.when(c != p)
        def _():
            for copy in core_copies(layer):
                copy.wait_recv()

        at(0)
        shifts = parbuf[layer, 0:1, :]
        scales = parbuf[layer, 1:2, :]
        gain = parbuf[layer, 3:4, 0:HEAD]
        for i in range(SLOTS):
            rows = pl.ds(i * chunk, chunk)
            numbers = hbuf[p, rows, :].astype(jnp.float32)
            average = jnp.mean(numbers, axis=-1, keepdims=True)
            centred = numbers - average
            spread = jnp.mean(centred * centred, axis=-1, keepdims=True)
            mod[rows, :] = (centred * lax.rsqrt(spread + EPS) * scales + shifts).astype(jnp.bfloat16)

        def kv_copy(j, kind):
            if kind == 0:
                ref = kvo.at[p, j, c]
                dst, device = ref, sib
            elif kind == 1:
                ref, dst, device = kvo.at[p, j, c], kvn.at[p, j, c, 0], t_next
            elif kind == 2:
                ref, dst, device = kvo.at[p, j, c], kvn.at[p, j, c, 1], t_prev
            else:
                ref = kvn.at[p, j, c, kind - 3]
                dst, device = ref, sib
            return remote(ref, dst, kv_s.at[p, j, kind], kv_r.at[p, j, kind], device)

        for j in range(heads):
            projected = dot(mod[...], wbuf[layer, :, 2 * HEAD * j : 2 * HEAD * (j + 1)])
            kvo[p, j, c, :, 0:HEAD] = head_norm(projected[:, 0:HEAD], gain)
            kvo[p, j, c, :, HEAD : 2 * HEAD] = projected[:, HEAD:].astype(jnp.bfloat16)
            for kind in (1, 2, 0):
                kv_copy(j, kind).start()
        at(1)
        queries = dot(mod[...], wbuf[layer, :, 2 * HEAD * heads :])
        query_gain = gain * (math.log2(math.e) / math.sqrt(HEAD))
        for j in range(heads):
            qbuf[j] = head_norm(queries[:, HEAD * j : HEAD * (j + 1)], query_gain)

        @pl.when(section == layer - 1)
        def _():
            keep_own().wait()

        @pl.when(2 * y + 1 - c == layer - 1)
        def _():
            keep_other().wait_send()

        for j in range(heads):
            kv_copy(j, 0).wait_recv()
            block = kvo[p, j].reshape(tokens, 2 * HEAD)
            acc[j] = one_block(j, block[:, 0:HEAD], block[:, HEAD:], bias[0])
        at(2)

        def near(j, side):
            block = kvn[p, j, side].reshape(tokens, 2 * HEAD)
            return one_block(j, block[:, 0:HEAD], block[:, HEAD:], bias[1 + side])

        def pass_on(j):
            for kind in (1, 2):
                kv_copy(j, kind).wait_recv()
            for kind in (3, 4):
                kv_copy(j, kind).start()
            acc[j] += near(j, c)

        def g_copy(j, d, back):
            place = (y + NY - d) % NY if back else y
            columns = pl.ds(pl.multiple_of((place * heads + j) * HEAD, HEAD), HEAD)
            ref = hbuf.at[q, :, columns]
            return remote(ref, ref, g_s.at[p, j, d - 1], g_r.at[p, j, d - 1], y_peer(d))

        def finish(j):
            for kind in (3, 4):
                kv_copy(j, kind).wait_recv()
            total = acc[j] + near(j, 1 - c)
            columns = pl.ds(pl.multiple_of((y * heads + j) * HEAD, HEAD), HEAD)
            attended = total[:, 0:HEAD] / total[:, HEAD:]
            gates = parbuf[layer, 2:3, columns]
            numbers = hbuf[p, :, columns].astype(jnp.float32) + gates * attended
            hbuf[q, :, columns] = numbers.astype(jnp.bfloat16)
            for d in (1, 3, 2):
                g_copy(j, d, False).start()

        pass_on(0)
        for j in range(1, heads):
            pass_on(j)
            if j == heads - 1:
                at(3)
            finish(j - 1)
        finish(heads - 1)
        at(4)
        for j in range(heads):
            for kind in range(5):
                kv_copy(j, kind).wait_send()
        for j in range(heads):
            for d in (1, 3, 2):
                g_copy(j, d, False).wait_send()
                g_copy(j, d, True).wait_recv()

        @pl.when(c == p)
        def _():
            for copy in core_copies(layer):
                copy.wait_send()

        @pl.when(section == layer)
        def _():
            keep_own().start()

        @pl.when(2 * y + 1 - c == layer)
        def _():
            keep_other().start()

        return carry

    def out_rows(place):
        return out.at[0, 0, pl.ds(pl.multiple_of(half * place, 16), half)]

    def keep_own():
        return pltpu.make_async_copy(hbuf.at[1 - c], out_rows(c), o_l.at[0])

    def keep_other():
        return remote(hbuf.at[c], out_rows(c), o_s.at[0], o_r.at[0], sib)

    lax.fori_loop(0, layers, layer_step, 0)

    @pl.when(section == layers - 1)
    def _():
        keep_own().wait()

    @pl.when(2 * y + 1 - c == layers - 1)
    def _():
        keep_other().wait_send()

    remote(hbuf.at[c], out_rows(1 - c), o_s.at[0], o_r.at[0], sib).wait_recv()


def allowed_bias(slot_tile, window_tiles, core, tokens):
    tiles = slot_tile.shape[0]
    tile_place = lax.axis_index("tile")
    tile_len = tokens // SLOTS
    half = tokens // 2
    slots = (tile_place * SLOTS + jnp.arange(-SLOTS, 2 * SLOTS, dtype=jnp.int32) + tiles) % tiles
    ids = jnp.sum(jnp.where(slots[:, None] == jnp.arange(tiles, dtype=jnp.int32)[None], slot_tile[None], 0), axis=1)
    own = ids[SLOTS : 2 * SLOTS]
    picked = own[:, None] == jnp.arange(tiles, dtype=jnp.int32)[None]
    listed = jnp.sum(jnp.where(picked[:, :, None], window_tiles[None], 0), axis=1)
    allowed = jnp.any(listed[:, :, None] == ids[None, None], axis=1)
    bias = jnp.where(allowed, 0.0, NEG).astype(jnp.float32)
    first, second = bias[jnp.array([0, 0, 1])], bias[jnp.array([1, 2, 2])]
    rows = jnp.where(core == 0, first, second)
    rows = jnp.repeat(rows.reshape(SLOTS, 3, SLOTS), tile_len, axis=2)
    blocks = [rows[:, 1]]
    for side in range(2):
        part = rows[:, :, side * half : (side + 1) * half]
        blocks.append(jnp.concatenate([part[:, 0], part[:, 2]], axis=1))
    return jnp.stack(blocks)[:, :, None, :]


def on_device(nx, latent, w_qkv, mod_shift, mod_scale, attn_gate, qk_gain, slot_tile, window_tiles):
    layers = lax.axis_size("section")
    n_tile = lax.axis_size("tile")
    nz = n_tile // nx
    _, tokens, width = latent.shape
    heads = width // HEAD // NY
    shard = w_qkv.shape[1]
    half = tokens // 2
    cols = 3 * heads * HEAD
    parts = w_qkv[0].reshape(shard, 3, NY, heads, HEAD)
    key_value = jnp.transpose(parts[:, 1:], (2, 0, 3, 1, 4)).reshape(NY, shard, 2 * heads * HEAD)
    query = jnp.transpose(parts[:, 0], (1, 0, 2, 3)).reshape(NY, shard, heads * HEAD)
    wp = jnp.concatenate([key_value, query], axis=-1)
    gain_row = jnp.pad(qk_gain, ((0, 0), (0, width - HEAD)))
    par = jnp.concatenate([mod_shift, mod_scale, attn_gate, gain_row, jnp.zeros((4, width), jnp.float32)], axis=0)
    bias = allowed_bias(slot_tile, window_tiles, lax.axis_index("section") % 2, tokens)
    pairs = layers // 2
    bf16, f32 = jnp.bfloat16, jnp.float32
    dma = pltpu.SemaphoreType.DMA
    any_space = pl.BlockSpec(memory_space=pl.ANY)
    return pl.pallas_call(
        functools.partial(kernel, layers, nx, nz, heads, tokens),
        out_shape=jax.ShapeDtypeStruct((1, 1, tokens, width), bf16),
        in_specs=[any_space, any_space, any_space, pl.BlockSpec(memory_space=pltpu.VMEM)],
        out_specs=any_space,
        scratch_shapes=[
            pltpu.VMEM((2, half, width), bf16),
            pltpu.VMEM((half, width), bf16),
            pltpu.VMEM((layers, width, cols), bf16),
            pltpu.VMEM((layers, 8, width), f32),
            pltpu.VMEM((heads, half, HEAD), bf16),
            pltpu.VMEM((2, heads, 2, half, 2 * HEAD), bf16),
            pltpu.VMEM((2, heads, 2, 2, half, 2 * HEAD), bf16),
            pltpu.VMEM((heads, half, 2 * HEAD), f32),
            dma((3,)), dma((3,)), dma((3,)), dma((3,)), dma((3,)),
            dma((pairs, 4, 2)), dma((pairs, 4, 2)), dma((pairs, 2, 2)), dma((pairs, 2, 2)),
            dma((pairs,)), dma((pairs,)), dma((pairs,)), dma((pairs,)),
            dma((2, heads, 5)), dma((2, heads, 5)), dma((2, heads, 3)), dma((2, heads, 3)),
            dma((1,)), dma((1,)), dma((1,)),
        ],
        compiler_params=pltpu.CompilerParams(
            collective_id=0, has_side_effects=True, vmem_limit_bytes=58 * 1024 * 1024
        ),
    )(latent, wp, par, bias)


def solution(mesh, nx=NX):
    return jax.shard_map(
        functools.partial(on_device, nx),
        mesh=mesh,
        in_specs=(
            P(None, "tile", None),
            P("section", "tile", None),
            P("section", None),
            P("section", None),
            P("section", None),
            P("section", None),
            P(),
            P(),
        ),
        out_specs=P("section", None, "tile", None),
        check_vma=False,
    )
```

time: 2120 us -> 309 us (0.15)
  waiting for transfers between devices: 1750 us -> 0 us
  Pallas kernels: 0 us -> 295 us
  other arithmetic: 141 us -> 4.35 us
  local copies, waits for them, and re-layouts: 123 us -> 9.65 us
  matrix products: 66.9 us -> 0 us
  starting transfers between devices: 22.5 us -> 0 us
    ppermute x24 -> x0, waiting for transfers between devices: 1620 us -> none  [the longest x8 1170 us: shifted(): return lax.ppermute(block, axis, route)]
    pallas_call x0 -> x1, Pallas kernels: none -> 295 us  [on_device(): pl.pallas_call(functools.partial(kernel, layers, nx, nz, heads, tokens),...]
    all_gather x1 -> x0, waiting for transfers between devices: 129 us -> none  [on_device(): whole_weights = lax.all_gather(weight_part, 'tile', axis=0, tiled=True)]
    concatenate x9 -> x1, other arithmetic: 74.9 us -> 0.8 us  [on_device(): wp = jnp.concatenate([key_value, query], axis=-1)]
    dot_general x25 -> x0, matrix products: 66.9 us -> none  [the longest x12 31.7 us: one_head(): jnp.einsum('gqk,gkd->gqd', probs, head_values, preferred_element_type=jnp...]
    another operation x23 -> x2, local copies, waits for them, and re-layouts: 47 us -> 1.75 us  [the longest x1 1.74 us: on_device(): parts = w_qkv[0].reshape(shard, 3, NY, heads, HEAD)]
    select_n x16 -> x3, other arithmetic: 43.4 us -> 0.03 us  [the longest x1 0.02 us: allowed_bias(): (tile_place * SLOTS + jnp.arange(-SLOTS, 2 * SLOTS, dtype=jnp.int32) + ti...]
    ppermute x24 -> x0, starting transfers between devices: 22.5 us -> none  [the longest x8 10.3 us: extended(): lax.ppermute(lax.slice_in_dim(block, block.shape[dim] - width, None, axis...]
  transfers between devices with their start and end apart: 25 -> 0, of which waited for: 25 -> 0; matrix products, arithmetic and copies ran while one was open for 0% -> 0% of each run, Pallas kernels for 0% -> 0%
where the time goes in v1:
time: 309 us
  Pallas kernels  295 us (95%)
  local copies, waits for them, and re-layouts  9.65 us (3%)
  other arithmetic  4.35 us (1%)
    pallas_call x1, Pallas kernels, on_device(): pl.pallas_call(functools.partial(kernel, layers, nx, nz, heads, tokens),...  295 us

profile of v1, /device:TPU:25, one launch (start us, length us, event | category | flops | bytes accessed | tf_op | source)
XLA Modules:
  0.0 309.0 jit_solution(6865124232449545459)
XLA Ops:
  0.0 0.8 select_reduce_fusion.1
  0.9 0.1 slice.32
  0.9 0.1 iota_compare_fusion.1
  1.0 0.9 select_reduce_fusion
  1.9 0.3 compare_reduce_fusion
  2.2 0.1 copy.21
  2.3 0.7 pad_clamp_fusion.1
  3.0 0.6 gather_fusion
  3.5 0.7 pad_clamp_fusion
  4.2 0.6 gather_fusion.1
  4.8 0.1 select_n.56
  4.9 0.7 pad.4
  5.5 1.4 concatenate.13.par
  7.0 0.1 reshape.53
  7.2 0.1 maximum_bitcast_fusion
  7.3 0.6 broadcast_in_dim.75.bias
  7.9 1.7 reshape_squeeze.3
  9.7 0.1 slice_bitcast_fusion
  9.9 0.3 copy.19
  10.2 0.1 reshape.70
  10.3 0.1 reshape.51
  10.5 0.8 pad_maximum_fusion.wp
  11.3 294.9 %shard_map.100 = bf16[1,1,576,1536]{3,2,1,0:T(8,128)(2,1)} custom-call(bf16[1,576,1536]{2,1,0:T(8,128)(2,1)} %lat.1, bf16[4,48,1152]{2,1,0:T(8,128)(2,1)} %pad_maximum_fusion.wp, f32[8,1536]{1,0:T(8,128)} %concatenate.13.par, f32[3,3,1,576]{3,2,1,0:T(1,128)} %broadcast_in_dim.75.bias), custom_call_target="tpu_custom_call" | custom-call | tf_op jit(solution)/shard_map/pallas_call | solution.py:380
  306.2 2.8 copy.25
  (11 shorter events, 0.3 us)

commit v2 on v1

v2 whole, which is shorter than its diff:
```python
import functools
import math

import jax
import jax.numpy as jnp
from jax import lax
from jax.experimental import pallas as pl
from jax.experimental.pallas import tpu as pltpu
from jax.sharding import PartitionSpec as P

MESH = pl.DeviceIdType.MESH
HEAD = 128
SLOTS = 3
NY = 4
NX = 4
EPS = 1e-06
NEG = -1e30


def kernel(
    layers, nx, nz, heads, tokens, lat, w_part, shift_row, scale_row, gate_row, gain_row, slot_ids, windows, out,
    hbuf, mod, wbuf, parbuf, qbuf, kvo, kvn, acc, bias,
    loc_sem, a2a_s, a2a_r, par_s, par_r, z_s, z_r, x0_s, x0_r, x_s, x_r, xf_s, xf_r, c_s, c_r, cp_s, cp_r,
    kv_s, kv_r, g_s, g_r, o_s, o_r, o_l,
):
    width = NY * heads * HEAD
    half = tokens // 2
    chunk = half // SLOTS
    shard = w_part.shape[1]
    group = heads * HEAD
    n_tile = nx * nz
    section = lax.axis_index("section")
    t = lax.axis_index("tile")
    y, c = section // 2, section % 2
    x, z = t // nz, t % nz
    sib = (2 * y + 1 - c, t)
    t_next = (section, (t + 1) % n_tile)
    t_prev = (section, (t + n_tile - 1) % n_tile)
    z_next = (section, x * nz + (z + 1) % nz)
    z_prev = (section, x * nz + (z + nz - 1) % nz)
    x_next = (section, ((x + 1) % nx) * nz + z)
    x_prev = (section, ((x + nx - 1) % nx) * nz + z)

    def y_peer(d):
        return (2 * ((y + d) % NY) + c, t)

    def remote(src, dst, send, recv, device):
        return pltpu.make_async_remote_copy(
            src_ref=src, dst_ref=dst, send_sem=send, recv_sem=recv, device_id=device, device_id_type=MESH
        )

    partners = [y_peer(1), y_peer(2), y_peer(3), sib, t_next, t_prev]
    if nz > 1:
        partners += [z_next, z_prev]
    if nx > 1:
        partners += [x_next, x_prev, (section, ((x + 2) % nx) * nz + z)]
    load_h = pltpu.make_async_copy(lat.at[0, pl.ds(pl.multiple_of(half * c, 16), half)], hbuf.at[0], loc_sem.at[0])
    load_h.start()
    own_rows = pl.ds(pl.multiple_of(shard * t, 16), shard)

    def w_slices(place):
        for i in range(3):
            start = pl.multiple_of(i * width + place * group, HEAD)
            yield w_part.at[0, :, pl.ds(start, group)], wbuf.at[section, own_rows, i * group : (i + 1) * group]

    own_shard = wbuf.at[section, own_rows]
    for src, dst in w_slices(y):
        pltpu.make_async_copy(src, dst, loc_sem.at[1]).start()
    parbuf[section] = jnp.zeros(parbuf.shape[1:], jnp.float32)
    for i, row in enumerate((shift_row, scale_row, gate_row)):
        parbuf[section, i : i + 1, :] = row[...]
    parbuf[section, 3:4, 0:HEAD] = gain_row[...]
    barrier = pltpu.get_barrier_semaphore()
    for device in partners:
        pl.semaphore_signal(barrier, inc=1, device_id=device, device_id_type=MESH)
    pl.semaphore_wait(barrier, len(partners))

    def a2a_start():
        for d in (1, 3, 2):
            for src, dst in w_slices((y + d) % NY):
                remote(src, dst, a2a_s.at[d - 1], a2a_r.at[d - 1], y_peer(d)).start()
            remote(parbuf.at[section], parbuf.at[section], par_s.at[d - 1], par_r.at[d - 1], y_peer(d)).start()

    def a2a_whole(d):
        return (
            remote(own_shard, own_shard, a2a_s.at[d - 1], a2a_r.at[d - 1], sib),
            remote(parbuf.at[section], parbuf.at[section], par_s.at[d - 1], par_r.at[d - 1], sib),
        )

    @pl.when(y == 0)
    def _():
        a2a_start()

    @pl.when(y != 0)
    def _():
        for copy in a2a_whole(y):
            copy.wait_recv()
        a2a_start()

    pltpu.make_async_copy(own_shard, own_shard, loc_sem.at[1]).wait()

    def a2a_finish():
        for d in (1, 2, 3):
            for copy in a2a_whole(d):
                copy.wait_send()

            @pl.when(d != y)
            def _():
                for copy in a2a_whole(d):
                    copy.wait_recv()

    def rows_of(xx, zz):
        return pl.ds(pl.multiple_of((xx * nz + zz) * shard, 16), shard)

    right_steps = nz // 2
    left_steps = (nz - 1) // 2

    def z_copy(layer, step, way):
        k = layer // 2
        zz = (z + nz - step) % nz if way == 0 else (z + step) % nz
        ref = wbuf.at[layer, rows_of(x, zz)]
        return remote(ref, ref, z_s.at[k, step, way], z_r.at[k, step, way], z_next if way == 0 else z_prev)

    def z_event(layer, step):
        if step > 0:
            if step - 1 < right_steps:
                z_copy(layer, step - 1, 0).wait()
            if step - 1 < left_steps:
                z_copy(layer, step - 1, 1).wait()
        if step < right_steps:
            z_copy(layer, step, 0).start()
        if step < left_steps:
            z_copy(layer, step, 1).start()

    z_events = right_steps + 1

    block = nz * shard

    def x_rows(place, piece=None):
        if piece is None:
            return pl.ds(pl.multiple_of(place * block, 16), block)
        return pl.ds(pl.multiple_of(place * block + piece * (block // 2), 16), block // 2)

    def x_copy(layer, way, order):
        ref = wbuf.at[layer, x_rows(x, order if way == 0 else 1 - order)]
        k = layer // 2
        return remote(ref, ref, x_s.at[k, way, order], x_r.at[k, way, order], x_next if way == 0 else x_prev)

    def x_forward(layer, way):
        place = (x + nx - 1) % nx if way == 0 else (x + 1) % nx
        ref = wbuf.at[layer, x_rows(place, way)]
        k = layer // 2
        return remote(ref, ref, xf_s.at[k, way], xf_r.at[k, way], x_next if way == 0 else x_prev)

    def core_copy(layer, d):
        k = layer // 2
        ref = wbuf.at[layer, x_rows((x + d) % nx)]
        return remote(ref, ref, c_s.at[k, d], c_r.at[k, d], sib)

    def core_par(layer):
        k = layer // 2
        return remote(parbuf.at[layer], parbuf.at[layer], cp_s.at[k], cp_r.at[k], sib)

    def x_event(layer, step):
        if step == 0:
            core_copy(layer, 0).start()
            core_par(layer).start()
        if nx == 1:
            return
        if step == 0:
            for order in range(2):
                for way in range(2):
                    x_copy(layer, way, order).start()
        elif step == 1:
            for way in range(2):
                x_copy(layer, way, 0).wait_recv()
                x_forward(layer, way).start()
        else:
            for way in range(2):
                x_copy(layer, way, 1).wait_recv()
                core_copy(layer, nx - 1 if way == 0 else 1).start()
            for way in range(2):
                x_forward(layer, way).wait_recv()
            core_copy(layer, 2).start()
            for way in range(2):
                x_copy(layer, way, 0).wait_send()
                x_copy(layer, way, 1).wait_send()
                x_forward(layer, way).wait_send()

    def x_direct(shards):
        for zz in shards:
            ref = wbuf.at[0, rows_of(x, zz % nz)]
            for d in (1, 3, 2) if nx == 4 else ():
                to = (section, ((x + d) % nx) * nz + z)
                remote(ref, ref, x0_s.at[d - 1], x0_r.at[d - 1], to).start()

    def x_direct_whole(d, back):
        ref = wbuf.at[0, x_rows((x + nx - d) % nx if back else x)]
        return remote(ref, ref, x0_s.at[d - 1], x0_r.at[d - 1], sib)

    @pl.when(c == 0)
    def _():
        x_direct([z])
        for step in range(z_events):
            z_event(0, step)
            if step > 0:
                fresh = []
                if step - 1 < right_steps:
                    fresh.append(z + nz - step)
                if step - 1 < left_steps:
                    fresh.append(z + step)
                x_direct(fresh)
        core_copy(0, 0).start()
        core_par(0).start()
        a2a_finish()
        z_event(2, 0)
        if nx > 1:
            for d in (1, 3, 2):
                x_direct_whole(d, True).wait_recv()
                core_copy(0, nx - d).start()
                if d == 3:
                    z_event(2, 1)
            for d in (1, 3, 2):
                x_direct_whole(d, False).wait_send()
        else:
            z_event(2, 1)
        if z_events > 2:
            z_event(2, 2)

    @pl.when(c == 1)
    def _():
        a2a_finish()
        core_copy(0, 0).wait_recv()
        core_par(0).wait_recv()
        for step in range(z_events):
            z_event(1, step)
        for d in range(1, nx):
            core_copy(0, d).wait_recv()
        x_event(1, 0)

    tile_len = tokens // SLOTS
    n_slots = n_tile * SLOTS
    lanes = lax.broadcasted_iota(jnp.int32, (1, tokens), 1)

    def penalty(query_slot, frame, key_slot):
        place = (t + n_tile + frame) % n_tile
        key_id = slot_ids[place * SLOTS + key_slot]
        row = windows[pl.ds(slot_ids[t * SLOTS + query_slot], 1), :]
        listed = jnp.max(jnp.where(row == key_id, 1.0, 0.0), axis=1, keepdims=True)
        return jnp.where(listed > 0.0, 0.0, NEG)

    for i in range(SLOTS):
        query_slot = (half * c + chunk * i) // tile_len
        table = [[penalty(query_slot, frame, k) for k in range(SLOTS)] for frame in (-1, 0, 1)]

        def spread_over(tokens_at, pens):
            return jnp.where(tokens_at < tile_len, pens[0], jnp.where(tokens_at < 2 * tile_len, pens[1], pens[2]))

        bias[0, i] = spread_over(lanes, table[1])
        for side in range(2):
            low = spread_over(lanes + side * half, table[0])
            high = spread_over(lanes - half + side * half, table[2])
            bias[1 + side, i] = jnp.where(lanes < half, low, high)

    load_h.wait()

    ones = jnp.ones((tokens, HEAD), jnp.bfloat16)

    def dot(a, b):
        return jnp.dot(a, b, preferred_element_type=jnp.float32)

    def head_norm(numbers, gain):
        square_mean = jnp.mean(numbers * numbers, axis=-1, keepdims=True)
        return (numbers * lax.rsqrt(square_mean + EPS) * gain).astype(jnp.bfloat16)

    def one_block(j, keys, values, allowed):
        scores = lax.dot_general(
            qbuf[j], keys, (((1,), (1,)), ((), ())), preferred_element_type=jnp.float32
        )
        scores = scores.reshape(SLOTS, chunk, tokens) + allowed
        powers = jnp.exp2(scores).astype(jnp.bfloat16).reshape(half, tokens)
        return dot(powers, jnp.concatenate([values, ones], axis=1))

    def layer_step(layer, carry):
        p = layer % 2
        q = 1 - p

        def event(ahead, condition, do):
            ours = jnp.logical_and((layer + ahead) % 2 == c, layer + ahead < layers)
            if condition is not None:
                ours = jnp.logical_and(ours, condition)

            @pl.when(ours)
            def _():
                do(layer + ahead)

        def z_at(ahead, step):
            if step < z_events:
                event(ahead, None, lambda target: z_event(target, step))

        def at(place):
            if place == 0:
                z_at(2, 3)
                event(1, layer > 0, lambda target: x_event(target, 1))
                z_at(3, 0)
            elif place == 1:
                z_at(2, 4)
                event(2, None, lambda target: x_event(target, 0))
                event(1, layer > 0, lambda target: x_event(target, 2))
                event(1, layer == 0, lambda target: x_event(target, 1))
                z_at(3, 1)
            else:
                event(1, layer == 0, lambda target: x_event(target, 2))
                z_at(3, 2)

        @pl.when(jnp.logical_and(c != p, layer > 0))
        def _():
            core_par(layer).wait_recv()
            for d in range(nx):
                core_copy(layer, d).wait_recv()

        shifts = parbuf[layer, 0:1, :]
        scales = parbuf[layer, 1:2, :]
        gain = parbuf[layer, 3:4, 0:HEAD]
        for i in range(SLOTS):
            rows = pl.ds(i * chunk, chunk)
            numbers = hbuf[p, rows, :].astype(jnp.float32)
            average = jnp.mean(numbers, axis=-1, keepdims=True)
            centred = numbers - average
            spread = jnp.mean(centred * centred, axis=-1, keepdims=True)
            mod[rows, :] = (centred * lax.rsqrt(spread + EPS) * scales + shifts).astype(jnp.bfloat16)

        def kv_copy(j, kind):
            if kind == 0:
                ref = kvo.at[p, j, c]
                dst, device = ref, sib
            elif kind == 1:
                ref, dst, device = kvo.at[p, j, c], kvn.at[p, j, c, 0], t_next
            elif kind == 2:
                ref, dst, device = kvo.at[p, j, c], kvn.at[p, j, c, 1], t_prev
            else:
                ref = kvn.at[p, j, c, kind - 3]
                dst, device = ref, sib
            return remote(ref, dst, kv_s.at[p, j, kind], kv_r.at[p, j, kind], device)

        for j in range(heads):
            weights = jnp.concatenate(
                [wbuf[layer, :, i * group + HEAD * j : i * group + HEAD * (j + 1)] for i in (1, 2)], axis=1
            )
            projected = dot(mod[...], weights)
            kvo[p, j, c, :, 0:HEAD] = head_norm(projected[:, 0:HEAD], gain)
            kvo[p, j, c, :, HEAD : 2 * HEAD] = projected[:, HEAD:].astype(jnp.bfloat16)
            for kind in (1, 2, 0):
                kv_copy(j, kind).start()
            if j == 0:
                at(0)
        queries = dot(mod[...], wbuf[layer, :, 0:group])
        query_gain = gain * (math.log2(math.e) / math.sqrt(HEAD))
        for j in range(heads):
            qbuf[j] = head_norm(queries[:, HEAD * j : HEAD * (j + 1)], query_gain)

        @pl.when(section == layer - 1)
        def _():
            keep_own().wait()

        @pl.when(2 * y + 1 - c == layer - 1)
        def _():
            keep_other().wait_send()

        for j in range(heads):
            kv_copy(j, 0).wait_recv()
            block = kvo[p, j].reshape(tokens, 2 * HEAD)
            acc[j] = one_block(j, block[:, 0:HEAD], block[:, HEAD:], bias[0])

        def near(j, side):
            block = kvn[p, j, side].reshape(tokens, 2 * HEAD)
            return one_block(j, block[:, 0:HEAD], block[:, HEAD:], bias[1 + side])

        def pass_on(j):
            for kind in (1, 2):
                kv_copy(j, kind).wait_recv()
                kv_copy(j, kind + 2).start()
            acc[j] += near(j, c)

        def g_copy(j, d, back):
            place = (y + NY - d) % NY if back else y
            columns = pl.ds(pl.multiple_of((place * heads + j) * HEAD, HEAD), HEAD)
            ref = hbuf.at[q, :, columns]
            return remote(ref, ref, g_s.at[p, j, d - 1], g_r.at[p, j, d - 1], y_peer(d))

        def sends_to(d):
            return jnp.logical_or(layer < layers - 1, (y + d) % NY == NY - 1)

        def finish(j):
            for kind in (3, 4):
                kv_copy(j, kind).wait_recv()
            total = acc[j] + near(j, 1 - c)
            columns = pl.ds(pl.multiple_of((y * heads + j) * HEAD, HEAD), HEAD)
            attended = total[:, 0:HEAD] / total[:, HEAD:]
            gates = parbuf[layer, 2:3, columns]
            numbers = hbuf[p, :, columns].astype(jnp.float32) + gates * attended
            hbuf[q, :, columns] = numbers.astype(jnp.bfloat16)
            for d in (1, 3, 2):

                @pl.when(sends_to(d))
                def _():
                    g_copy(j, d, False).start()

        for j in range(heads):
            pass_on(j)
            finish(j)
            if j == 0:
                at(1)
        at(2)
        for j in range(heads):
            for kind in range(5):
                kv_copy(j, kind).wait_send()
        for d in (1, 3, 2):

            @pl.when(sends_to(d))
            def _():
                for j in range(heads):
                    g_copy(j, d, False).wait_send()

        @pl.when(sends_to(0))
        def _():
            for j in range(heads):
                for d in (1, 3, 2):
                    g_copy(j, d, True).wait_recv()

        @pl.when(c == p)
        def _():
            core_par(layer).wait_send()
            for d in range(nx):
                core_copy(layer, d).wait_send()

        @pl.when(section == layer)
        def _():
            keep_own().start()

        @pl.when(2 * y + 1 - c == layer)
        def _():
            keep_other().start()

        return carry

    def out_rows(place):
        return out.at[0, 0, pl.ds(pl.multiple_of(half * place, 16), half)]

    def keep_own():
        return pltpu.make_async_copy(hbuf.at[1 - c], out_rows(c), o_l.at[0])

    def keep_other():
        return remote(hbuf.at[c], out_rows(c), o_s.at[0], o_r.at[0], sib)

    lax.fori_loop(0, layers, layer_step, 0)

    @pl.when(section == layers - 1)
    def _():
        keep_own().wait()

    @pl.when(2 * y + 1 - c == layers - 1)
    def _():
        keep_other().wait_send()

    remote(hbuf.at[c], out_rows(1 - c), o_s.at[0], o_r.at[0], sib).wait_recv()


def on_device(nx, latent, w_qkv, mod_shift, mod_scale, attn_gate, qk_gain, slot_tile, window_tiles):
    layers = lax.axis_size("section")
    n_tile = lax.axis_size("tile")
    nz = n_tile // nx
    _, tokens, width = latent.shape
    heads = width // HEAD // NY
    shard = w_qkv.shape[1]
    half = tokens // 2
    cols = 3 * heads * HEAD
    pairs = layers // 2
    bf16, f32 = jnp.bfloat16, jnp.float32
    dma = pltpu.SemaphoreType.DMA
    any_space = pl.BlockSpec(memory_space=pl.ANY)
    in_vmem = pl.BlockSpec(memory_space=pltpu.VMEM)
    return pl.pallas_call(
        functools.partial(kernel, layers, nx, nz, heads, tokens),
        out_shape=jax.ShapeDtypeStruct((1, 1, tokens, width), bf16),
        in_specs=[any_space, any_space] + [in_vmem] * 4 + [pl.BlockSpec(memory_space=pltpu.SMEM), in_vmem],
        out_specs=any_space,
        scratch_shapes=[
            pltpu.VMEM((2, half, width), bf16),
            pltpu.VMEM((half, width), bf16),
            pltpu.VMEM((layers, width, cols), bf16),
            pltpu.VMEM((layers, 8, width), f32),
            pltpu.VMEM((heads, half, HEAD), bf16),
            pltpu.VMEM((2, heads, 2, half, 2 * HEAD), bf16),
            pltpu.VMEM((2, heads, 2, 2, half, 2 * HEAD), bf16),
            pltpu.VMEM((heads, half, 2 * HEAD), f32),
            pltpu.VMEM((3, SLOTS, 1, tokens), f32),
            dma((3,)), dma((3,)), dma((3,)), dma((3,)), dma((3,)),
            dma((pairs, 4, 2)), dma((pairs, 4, 2)), dma((3,)), dma((3,)),
            dma((pairs, 2, 2)), dma((pairs, 2, 2)), dma((pairs, 2)), dma((pairs, 2)),
            dma((pairs, 4)), dma((pairs, 4)), dma((pairs,)), dma((pairs,)),
            dma((2, heads, 5)), dma((2, heads, 5)), dma((2, heads, 3)), dma((2, heads, 3)),
            dma((1,)), dma((1,)), dma((1,)),
        ],
        compiler_params=pltpu.CompilerParams(
            collective_id=0, has_side_effects=True, vmem_limit_bytes=58 * 1024 * 1024
        ),
    )(latent, w_qkv, mod_shift, mod_scale, attn_gate, qk_gain, slot_tile, window_tiles)


def solution(mesh, nx=NX):
    return jax.shard_map(
        functools.partial(on_device, nx),
        mesh=mesh,
        in_specs=(
            P(None, "tile", None),
            P("section", "tile", None),
            P("section", None),
            P("section", None),
            P("section", None),
            P("section", None),
            P(),
            P(),
        ),
        out_specs=P("section", None, "tile", None),
        check_vma=False,
    )
```

time: 309 us -> 293 us (0.948)
  Pallas kernels: 295 us -> 289 us
  local copies, waits for them, and re-layouts: 9.65 us -> 4.23 us
  other arithmetic: 4.35 us -> 0 us
    pallas_call x1, Pallas kernels: 295 us -> 289 us  [on_device(): pl.pallas_call(functools.partial(kernel, layers, nx, nz, heads, tokens),...]
where the time goes in v2:
time: 293 us
  Pallas kernels  289 us (99%)
  local copies, waits for them, and re-layouts  4.23 us (1%)
    pallas_call x1, Pallas kernels, on_device(): pl.pallas_call(functools.partial(kernel, layers, nx, nz, heads, tokens),...  289 us

profile of v2, /device:TPU:25, one launch (start us, length us, event | category | flops | bytes accessed | tf_op | source)
XLA Modules:
  0.0 292.8 jit_solution(8182172669900917013)
XLA Ops:
  0.0 1.4 copy.9.windows
  1.4 288.5 %shard_map.82 = bf16[1,1,576,1536]{3,2,1,0:T(8,128)(2,1)} custom-call(bf16[1,576,1536]{2,1,0:T(8,128)(2,1)} %lat.1, bf16[1,48,4608]{2,1,0:T(8,128)(2,1)} %w_part.1, f32[1,1536]{1,0:T(1,128)} %shift_row.1, f32[1,1536]{1,0:T(1,128)} %scale_row.1, f32[1,1536]{1,0:T(1,128)} %gate_row.1, f32[1,128]{1,0:T(1,128)} %gain_row.1, s32[96]{0:T(128)} %slot_ids.1, ...), custom_call_target="tpu_custom_call" | custom-call | tf_op jit(solution)/shard_map/pallas_call | solution.py:483
  290.0 2.8 copy.11

commit v3 on v2

--- a/solution.py
+++ b/solution.py
@@ -36,13 +36,18 @@
     sib = (2 * y + 1 - c, t)
     t_next = (section, (t + 1) % n_tile)
     t_prev = (section, (t + n_tile - 1) % n_tile)
-    z_next = (section, x * nz + (z + 1) % nz)
-    z_prev = (section, x * nz + (z + nz - 1) % nz)
     x_next = (section, ((x + 1) % nx) * nz + z)
     x_prev = (section, ((x + nx - 1) % nx) * nz + z)
 
     def y_peer(d):
         return (2 * ((y + d) % NY) + c, t)
+
+    z_order = []
+    for d in range(1, nz // 2 + 1):
+        z_order += [d] if 2 * d == nz else [d, nz - d]
+
+    def z_peer(d):
+        return (section, x * nz + (z + d) % nz)
 
     def remote(src, dst, send, recv, device):
         return pltpu.make_async_remote_copy(
@@ -50,8 +55,7 @@
         )
 
     partners = [y_peer(1), y_peer(2), y_peer(3), sib, t_next, t_prev]
-    if nz > 1:
-        partners += [z_next, z_prev]
+    partners += [z_peer(d) for d in z_order]
     if nx > 1:
         partners += [x_next, x_prev, (section, ((x + 2) % nx) * nz + z)]
     load_h = pltpu.make_async_copy(lat.at[0, pl.ds(pl.multiple_of(half * c, 16), half)], hbuf.at[0], loc_sem.at[0])
@@ -112,27 +116,20 @@
     def rows_of(xx, zz):
         return pl.ds(pl.multiple_of((xx * nz + zz) * shard, 16), shard)
 
-    right_steps = nz // 2
-    left_steps = (nz - 1) // 2
-
-    def z_copy(layer, step, way):
+    def z_copy(layer, d, back=False):
         k = layer // 2
-        zz = (z + nz - step) % nz if way == 0 else (z + step) % nz
-        ref = wbuf.at[layer, rows_of(x, zz)]
-        return remote(ref, ref, z_s.at[k, step, way], z_r.at[k, step, way], z_next if way == 0 else z_prev)
-
-    def z_event(layer, step):
-        if step > 0:
-            if step - 1 < right_steps:
-                z_copy(layer, step - 1, 0).wait()
-            if step - 1 < left_steps:
-                z_copy(layer, step - 1, 1).wait()
-        if step < right_steps:
-            z_copy(layer, step, 0).start()
-        if step < left_steps:
-            z_copy(layer, step, 1).start()
-
-    z_events = right_steps + 1
+        ref = wbuf.at[layer, rows_of(x, (z + nz - d) % nz if back else z)]
+        return remote(ref, ref, z_s.at[k, d - 1], z_r.at[k, d - 1], z_peer(d))
+
+    def z_start(layer, order=None):
+        for d in z_order if order is None else order:
+            z_copy(layer, d).start()
+
+    def z_finish(layer):
+        for d in z_order:
+            z_copy(layer, d, True).wait_recv()
+        for d in z_order:
+            z_copy(layer, d).wait_send()
 
     block = nz * shard
 
@@ -162,7 +159,7 @@
         return remote(parbuf.at[layer], parbuf.at[layer], cp_s.at[k], cp_r.at[k], sib)
 
     def x_event(layer, step):
-        if step == 0:
+        if step == 2:
             core_copy(layer, 0).start()
             core_par(layer).start()
         if nx == 1:
@@ -187,12 +184,11 @@
                 x_copy(layer, way, 1).wait_send()
                 x_forward(layer, way).wait_send()
 
-    def x_direct(shards):
-        for zz in shards:
-            ref = wbuf.at[0, rows_of(x, zz % nz)]
-            for d in (1, 3, 2) if nx == 4 else ():
-                to = (section, ((x + d) % nx) * nz + z)
-                remote(ref, ref, x0_s.at[d - 1], x0_r.at[d - 1], to).start()
+    def x_direct(zz):
+        ref = wbuf.at[0, rows_of(x, zz)]
+        for d in (1, 3, 2) if nx == 4 else ():
+            to = (section, ((x + d) % nx) * nz + z)
+            remote(ref, ref, x0_s.at[d - 1], x0_r.at[d - 1], to).start()
 
     def x_direct_whole(d, back):
         ref = wbuf.at[0, x_rows((x + nx - d) % nx if back else x)]
@@ -200,42 +196,33 @@
 
     @pl.when(c == 0)
     def _():
-        x_direct([z])
-        for step in range(z_events):
-            z_event(0, step)
-            if step > 0:
-                fresh = []
-                if step - 1 < right_steps:
-                    fresh.append(z + nz - step)
-                if step - 1 < left_steps:
-                    fresh.append(z + step)
-                x_direct(fresh)
+        z_start(0)
+        x_direct(z)
+        for d in z_order:
+            z_copy(0, d, True).wait_recv()
+            x_direct((z + nz - d) % nz)
         core_copy(0, 0).start()
         core_par(0).start()
+        for d in z_order:
+            z_copy(0, d).wait_send()
         a2a_finish()
-        z_event(2, 0)
+        z_start(2)
         if nx > 1:
             for d in (1, 3, 2):
                 x_direct_whole(d, True).wait_recv()
                 core_copy(0, nx - d).start()
-                if d == 3:
-                    z_event(2, 1)
             for d in (1, 3, 2):
                 x_direct_whole(d, False).wait_send()
-        else:
-            z_event(2, 1)
-        if z_events > 2:
-            z_event(2, 2)
 
     @pl.when(c == 1)
     def _():
+        z_start(1)
         a2a_finish()
         core_copy(0, 0).wait_recv()
         core_par(0).wait_recv()
-        for step in range(z_events):
-            z_event(1, step)
         for d in range(1, nx):
             core_copy(0, d).wait_recv()
+        z_finish(1)
         x_event(1, 0)
 
     tile_len = tokens // SLOTS
@@ -294,24 +281,19 @@
             def _():
                 do(layer + ahead)
 
-        def z_at(ahead, step):
-            if step < z_events:
-                event(ahead, None, lambda target: z_event(target, step))
+        def z_then_x(target):
+            z_finish(target)
+            x_event(target, 0)
 
         def at(place):
             if place == 0:
-                z_at(2, 3)
                 event(1, layer > 0, lambda target: x_event(target, 1))
-                z_at(3, 0)
-            elif place == 1:
-                z_at(2, 4)
-                event(2, None, lambda target: x_event(target, 0))
-                event(1, layer > 0, lambda target: x_event(target, 2))
+            if place == 1:
                 event(1, layer == 0, lambda target: x_event(target, 1))
-                z_at(3, 1)
-            else:
-                event(1, layer == 0, lambda target: x_event(target, 2))
-                z_at(3, 2)
+                event(2, None, z_then_x)
+            if place == 2:
+                event(3, None, z_start)
+                event(1, None, lambda target: x_event(target, 2))
 
         @pl.when(jnp.logical_and(c != p, layer > 0))
         def _():
@@ -352,8 +334,7 @@
             kvo[p, j, c, :, HEAD : 2 * HEAD] = projected[:, HEAD:].astype(jnp.bfloat16)
             for kind in (1, 2, 0):
                 kv_copy(j, kind).start()
-            if j == 0:
-                at(0)
+        at(0)
         queries = dot(mod[...], wbuf[layer, :, 0:group])
         query_gain = gain * (math.log2(math.e) / math.sqrt(HEAD))
         for j in range(heads):
@@ -496,7 +477,7 @@
             pltpu.VMEM((heads, half, 2 * HEAD), f32),
             pltpu.VMEM((3, SLOTS, 1, tokens), f32),
             dma((3,)), dma((3,)), dma((3,)), dma((3,)), dma((3,)),
-            dma((pairs, 4, 2)), dma((pairs, 4, 2)), dma((3,)), dma((3,)),
+            dma((pairs, 8)), dma((pairs, 8)), dma((3,)), dma((3,)),
             dma((pairs, 2, 2)), dma((pairs, 2, 2)), dma((pairs, 2)), dma((pairs, 2)),
             dma((pairs, 4)), dma((pairs, 4)), dma((pairs,)), dma((pairs,)),
             dma((2, heads, 5)), dma((2, heads, 5)), dma((2, heads, 3)), dma((2, heads, 3)),

time: 293 us -> 259 us (0.88)
  Pallas kernels: 289 us -> 255 us
    pallas_call x1, Pallas kernels: 289 us -> 255 us  [on_device(): pl.pallas_call(functools.partial(kernel, layers, nx, nz, heads, tokens),...]
where the time goes in v3:
time: 259 us
  Pallas kernels  255 us (98%)
  local copies, waits for them, and re-layouts  4.23 us (2%)
    pallas_call x1, Pallas kernels, on_device(): pl.pallas_call(functools.partial(kernel, layers, nx, nz, heads, tokens),...  255 us

profile of v3, /device:TPU:25, one launch (start us, length us, event | category | flops | bytes accessed | tf_op | source)
XLA Modules:
  0.0 259.1 jit_solution(9449038813440864337)
XLA Ops:
  0.0 1.4 copy.9.windows
  1.4 254.9 %shard_map.82 = bf16[1,1,576,1536]{3,2,1,0:T(8,128)(2,1)} custom-call(bf16[1,576,1536]{2,1,0:T(8,128)(2,1)} %lat.1, bf16[1,48,4608]{2,1,0:T(8,128)(2,1)} %w_part.1, f32[1,1536]{1,0:T(1,128)} %shift_row.1, f32[1,1536]{1,0:T(1,128)} %scale_row.1, f32[1,1536]{1,0:T(1,128)} %gate_row.1, f32[1,128]{1,0:T(1,128)} %gain_row.1, s32[96]{0:T(128)} %slot_ids.1, ...), custom_call_target="tpu_custom_call" | custom-call | tf_op jit(solution)/shard_map/pallas_call | solution.py:464
  256.3 2.8 %copy.11 = bf16[1,1,576,1536]{3,2,1,0:T(8,128)(2,1)} copy(bf16[1,1,576,1536]{3,2,1,0:T(8,128)(2,1)} %shard_map.82) | data formatting | bytes 3538944

commit v4 on v3

--- a/solution.py
+++ b/solution.py
@@ -143,11 +143,27 @@
         k = layer // 2
         return remote(ref, ref, x_s.at[k, way, order], x_r.at[k, way, order], x_next if way == 0 else x_prev)
 
-    def x_forward(layer, way):
+    def x_forward(layer, part, way):
         place = (x + nx - 1) % nx if way == 0 else (x + 1) % nx
-        ref = wbuf.at[layer, x_rows(place, way)]
+        ref = wbuf.at[layer, x_rows(place, part)]
         k = layer // 2
-        return remote(ref, ref, xf_s.at[k, way], xf_r.at[k, way], x_next if way == 0 else x_prev)
+        return remote(ref, ref, xf_s.at[k, part], xf_r.at[k, part], x_next if way == 0 else x_prev)
+
+    def x_forward_early(layer):
+        for way in range(2 if nx > 1 else 0):
+            x_copy(layer, way, 0).wait_recv()
+
+            @pl.when(z != (0 if way == 0 else nz - 1))
+            def _():
+                x_forward(layer, way, way).start()
+
+    def x_forward_late(layer):
+        for way in range(2 if nx > 1 else 0):
+
+            @pl.when(z == (nz - 1 if way == 0 else 0))
+            def _():
+                x_copy(layer, way, 1).wait_recv()
+                x_forward(layer, 1 - way, way).start()
 
     def core_copy(layer, d):
         k = layer // 2
@@ -158,31 +174,36 @@
         k = layer // 2
         return remote(parbuf.at[layer], parbuf.at[layer], cp_s.at[k], cp_r.at[k], sib)
 
-    def x_event(layer, step):
-        if step == 2:
-            core_copy(layer, 0).start()
-            core_par(layer).start()
-        if nx == 1:
-            return
-        if step == 0:
+    def x_event(layer):
+        if nx > 1:
             for order in range(2):
                 for way in range(2):
                     x_copy(layer, way, order).start()
-        elif step == 1:
+
+    def core_first(layer):
+        core_copy(layer, 0).start()
+        core_par(layer).start()
+
+    def core_second(layer):
+        if nx > 1:
             for way in range(2):
-                x_copy(layer, way, 0).wait_recv()
-                x_forward(layer, way).start()
-        else:
-            for way in range(2):
-                x_copy(layer, way, 1).wait_recv()
+
+                @pl.when(z != (nz - 1 if way == 0 else 0))
+                def _():
+                    x_copy(layer, way, 1).wait_recv()
+
                 core_copy(layer, nx - 1 if way == 0 else 1).start()
-            for way in range(2):
-                x_forward(layer, way).wait_recv()
+
+    def core_last(layer):
+        if nx > 1:
+            for part in range(2):
+                x_forward(layer, part, 0).wait_recv()
             core_copy(layer, 2).start()
-            for way in range(2):
-                x_copy(layer, way, 0).wait_send()
-                x_copy(layer, way, 1).wait_send()
-                x_forward(layer, way).wait_send()
+            for part in range(2):
+                x_copy(layer, 0, part).wait_send()
+                x_copy(layer, 1, part).wait_send()
+            for part in range(2):
+                x_forward(layer, part, 0).wait_send()
 
     def x_direct(zz):
         ref = wbuf.at[0, rows_of(x, zz)]
@@ -206,7 +227,6 @@
         for d in z_order:
             z_copy(0, d).wait_send()
         a2a_finish()
-        z_start(2)
         if nx > 1:
             for d in (1, 3, 2):
                 x_direct_whole(d, True).wait_recv()
@@ -216,24 +236,24 @@
 
     @pl.when(c == 1)
     def _():
-        z_start(1)
         a2a_finish()
         core_copy(0, 0).wait_recv()
         core_par(0).wait_recv()
+        z_start(1)
         for d in range(1, nx):
             core_copy(0, d).wait_recv()
-        z_finish(1)
-        x_event(1, 0)
 
     tile_len = tokens // SLOTS
     n_slots = n_tile * SLOTS
     lanes = lax.broadcasted_iota(jnp.int32, (1, tokens), 1)
 
+    tile_lanes = lax.broadcasted_iota(jnp.int32, windows.shape, 1)
+
     def penalty(query_slot, frame, key_slot):
         place = (t + n_tile + frame) % n_tile
         key_id = slot_ids[place * SLOTS + key_slot]
-        row = windows[pl.ds(slot_ids[t * SLOTS + query_slot], 1), :]
-        listed = jnp.max(jnp.where(row == key_id, 1.0, 0.0), axis=1, keepdims=True)
+        in_window = jnp.logical_and(tile_lanes == slot_ids[t * SLOTS + query_slot], windows[...] == key_id)
+        listed = jnp.max(jnp.where(in_window, 1.0, 0.0), axis=(0, 1), keepdims=True)
         return jnp.where(listed > 0.0, 0.0, NEG)
 
     for i in range(SLOTS):
@@ -283,17 +303,34 @@
 
         def z_then_x(target):
             z_finish(target)
-            x_event(target, 0)
+            x_event(target)
+
+        def middle(target):
+            x_forward_late(target)
+            core_second(target)
+
+        def first_end(target):
+            x_forward_late(target)
+            core_first(target)
+            core_second(target)
 
         def at(place):
             if place == 0:
-                event(1, layer > 0, lambda target: x_event(target, 1))
-            if place == 1:
-                event(1, layer == 0, lambda target: x_event(target, 1))
-                event(2, None, z_then_x)
-            if place == 2:
+                event(1, layer == 0, z_then_x)
+                event(1, layer > 1, x_forward_early)
+                event(1, layer > 1, core_first)
+            elif place == 1:
+                event(1, layer > 1, middle)
+            elif place == 2:
+                event(1, layer <= 1, x_forward_early)
+                event(2, layer > 0, z_then_x)
+                event(2, layer == 0, z_start)
+            elif place == 3:
                 event(3, None, z_start)
-                event(1, None, lambda target: x_event(target, 2))
+            else:
+                event(1, layer <= 1, first_end)
+                event(1, None, core_last)
+                event(2, layer == 0, z_then_x)
 
         @pl.when(jnp.logical_and(c != p, layer > 0))
         def _():
@@ -352,6 +389,7 @@
             kv_copy(j, 0).wait_recv()
             block = kvo[p, j].reshape(tokens, 2 * HEAD)
             acc[j] = one_block(j, block[:, 0:HEAD], block[:, HEAD:], bias[0])
+        at(1)
 
         def near(j, side):
             block = kvn[p, j, side].reshape(tokens, 2 * HEAD)
@@ -389,10 +427,12 @@
 
         for j in range(heads):
             pass_on(j)
+            if j == heads - 1:
+                at(3)
             finish(j)
             if j == 0:
-                at(1)
-        at(2)
+                at(2)
+        at(4)
         for j in range(heads):
             for kind in range(5):
                 kv_copy(j, kind).wait_send()
@@ -486,7 +526,7 @@
         compiler_params=pltpu.CompilerParams(
             collective_id=0, has_side_effects=True, vmem_limit_bytes=58 * 1024 * 1024
         ),
-    )(latent, w_qkv, mod_shift, mod_scale, attn_gate, qk_gain, slot_tile, window_tiles)
+    )(latent, w_qkv, mod_shift, mod_scale, attn_gate, qk_gain, slot_tile, window_tiles.T)
 
 
 def solution(mesh, nx=NX):

time: 259 us -> 249 us (0.961)
  Pallas kernels: 255 us -> 246 us
    pallas_call x1, Pallas kernels: 255 us -> 246 us  [on_device(): pl.pallas_call(functools.partial(kernel, layers, nx, nz, heads, tokens),...]
where the time goes in v4:
time: 249 us
  Pallas kernels  246 us (99%)
  local copies, waits for them, and re-layouts  2.8 us (1%)
    pallas_call x1, Pallas kernels, on_device(): pl.pallas_call(functools.partial(kernel, layers, nx, nz, heads, tokens),...  246 us

profile of v4, /device:TPU:25, one launch (start us, length us, event | category | flops | bytes accessed | tf_op | source)
XLA Modules:
  0.0 249.3 jit_solution(1407162745904735208)
XLA Ops:
  0.0 246.5 %shard_map.82 = bf16[1,1,576,1536]{3,2,1,0:T(8,128)(2,1)} custom-call(bf16[1,576,1536]{2,1,0:T(8,128)(2,1)} %lat.1, bf16[1,48,4608]{2,1,0:T(8,128)(2,1)} %w_part.1, f32[1,1536]{1,0:T(1,128)} %shift_row.1, f32[1,1536]{1,0:T(1,128)} %scale_row.1, f32[1,1536]{1,0:T(1,128)} %gate_row.1, f32[1,128]{1,0:T(1,128)} %gain_row.1, s32[96]{0:T(128)} %slot_ids.1, ...), custom_call_target="tpu_custom_call" | custom-call | tf_op jit(solution)/shard_map/pallas_call | solution.py:504
  246.5 2.8 %copy.10 = bf16[1,1,576,1536]{3,2,1,0:T(8,128)(2,1)} copy(bf16[1,1,576,1536]{3,2,1,0:T(8,128)(2,1)} %shard_map.82) | data formatting | bytes 3538944

commit v5 on v4

--- a/solution.py
+++ b/solution.py
@@ -426,9 +426,9 @@
                     g_copy(j, d, False).start()
 
         for j in range(heads):
-            pass_on(j)
             if j == heads - 1:
                 at(3)
+            pass_on(j)
             finish(j)
             if j == 0:
                 at(2)

time: 249 us -> 247 us (level)
    pallas_call x1, Pallas kernels: 246 us -> 244 us  [on_device(): pl.pallas_call(functools.partial(kernel, layers, nx, nz, heads, tokens),...]
where the time goes in v5:
time: 247 us
  Pallas kernels  244 us (99%)
  local copies, waits for them, and re-layouts  2.8 us (1%)
    pallas_call x1, Pallas kernels, on_device(): pl.pallas_call(functools.partial(kernel, layers, nx, nz, heads, tokens),...  244 us

profile of v5, /device:TPU:25, one launch (start us, length us, event | category | flops | bytes accessed | tf_op | source)
XLA Modules:
  0.0 246.8 jit_solution(5821159656659895215)
XLA Ops:
  0.0 243.9 %shard_map.82 = bf16[1,1,576,1536]{3,2,1,0:T(8,128)(2,1)} custom-call(bf16[1,576,1536]{2,1,0:T(8,128)(2,1)} %lat.1, bf16[1,48,4608]{2,1,0:T(8,128)(2,1)} %w_part.1, f32[1,1536]{1,0:T(1,128)} %shift_row.1, f32[1,1536]{1,0:T(1,128)} %scale_row.1, f32[1,1536]{1,0:T(1,128)} %gate_row.1, f32[1,128]{1,0:T(1,128)} %gain_row.1, s32[96]{0:T(128)} %slot_ids.1, ...), custom_call_target="tpu_custom_call" | custom-call | tf_op jit(solution)/shard_map/pallas_call | solution.py:504
  244.0 2.8 %copy.10 = bf16[1,1,576,1536]{3,2,1,0:T(8,128)(2,1)} copy(bf16[1,1,576,1536]{3,2,1,0:T(8,128)(2,1)} %shard_map.82) | data formatting | bytes 3538944

commit v6 on v5

--- a/solution.py
+++ b/solution.py
@@ -227,6 +227,35 @@
         for d in z_order:
             z_copy(0, d).wait_send()
         a2a_finish()
+
+    tile_len = tokens // SLOTS
+    n_slots = n_tile * SLOTS
+    lanes = lax.broadcasted_iota(jnp.int32, (1, tokens), 1)
+
+    tile_lanes = lax.broadcasted_iota(jnp.int32, windows.shape, 1)
+
+    def penalty(query_slot, frame, key_slot):
+        place = (t + n_tile + frame) % n_tile
+        key_id = slot_ids[place * SLOTS + key_slot]
+        in_window = jnp.logical_and(tile_lanes == slot_ids[t * SLOTS + query_slot], windows[...] == key_id)
+        listed = jnp.max(jnp.where(in_window, 1.0, 0.0), axis=(0, 1), keepdims=True)
+        return jnp.where(listed > 0.0, 0.0, NEG)
+
+    for i in range(SLOTS):
+        query_slot = (half * c + chunk * i) // tile_len
+        table = [[penalty(query_slot, frame, k) for k in range(SLOTS)] for frame in (-1, 0, 1)]
+
+        def spread_over(tokens_at, pens):
+            return jnp.where(tokens_at < tile_len, pens[0], jnp.where(tokens_at < 2 * tile_len, pens[1], pens[2]))
+
+        bias[0, i] = spread_over(lanes, table[1])
+        for side in range(2):
+            low = spread_over(lanes + side * half, table[0])
+            high = spread_over(lanes - half + side * half, table[2])
+            bias[1 + side, i] = jnp.where(lanes < half, low, high)
+
+    @pl.when(c == 0)
+    def _():
         if nx > 1:
             for d in (1, 3, 2):
                 x_direct_whole(d, True).wait_recv()
@@ -242,32 +271,6 @@
         z_start(1)
         for d in range(1, nx):
             core_copy(0, d).wait_recv()
-
-    tile_len = tokens // SLOTS
-    n_slots = n_tile * SLOTS
-    lanes = lax.broadcasted_iota(jnp.int32, (1, tokens), 1)
-
-    tile_lanes = lax.broadcasted_iota(jnp.int32, windows.shape, 1)
-
-    def penalty(query_slot, frame, key_slot):
-        place = (t + n_tile + frame) % n_tile
-        key_id = slot_ids[place * SLOTS + key_slot]
-        in_window = jnp.logical_and(tile_lanes == slot_ids[t * SLOTS + query_slot], windows[...] == key_id)
-        listed = jnp.max(jnp.where(in_window, 1.0, 0.0), axis=(0, 1), keepdims=True)
-        return jnp.where(listed > 0.0, 0.0, NEG)
-
-    for i in range(SLOTS):
-        query_slot = (half * c + chunk * i) // tile_len
-        table = [[penalty(query_slot, frame, k) for k in range(SLOTS)] for frame in (-1, 0, 1)]
-
-        def spread_over(tokens_at, pens):
-            return jnp.where(tokens_at < tile_len, pens[0], jnp.where(tokens_at < 2 * tile_len, pens[1], pens[2]))
-
-        bias[0, i] = spread_over(lanes, table[1])
-        for side in range(2):
-            low = spread_over(lanes + side * half, table[0])
-            high = spread_over(lanes - half + side * half, table[2])
-            bias[1 + side, i] = jnp.where(lanes < half, low, high)
 
     load_h.wait()
 

time: 247 us -> 259 us (1.049)
  Pallas kernels: 244 us -> 256 us
    pallas_call x1, Pallas kernels: 244 us -> 256 us  [on_device(): pl.pallas_call(functools.partial(kernel, layers, nx, nz, heads, tokens),...]
where the time goes in v6:
time: 259 us; the launch traced here: 258 us
  Pallas kernels  256 us (99%)
  local copies, waits for them, and re-layouts  2.8 us (1%)
    pallas_call x1, Pallas kernels, on_device(): pl.pallas_call(functools.partial(kernel, layers, nx, nz, heads, tokens),...  256 us

profile of v6, /device:TPU:25, one launch (start us, length us, event | category | flops | bytes accessed | tf_op | source)
XLA Modules:
  0.0 258.4 jit_solution(12446866878545853063)
XLA Ops:
  0.0 255.6 %shard_map.82 = bf16[1,1,576,1536]{3,2,1,0:T(8,128)(2,1)} custom-call(bf16[1,576,1536]{2,1,0:T(8,128)(2,1)} %lat.1, bf16[1,48,4608]{2,1,0:T(8,128)(2,1)} %w_part.1, f32[1,1536]{1,0:T(1,128)} %shift_row.1, f32[1,1536]{1,0:T(1,128)} %scale_row.1, f32[1,1536]{1,0:T(1,128)} %gate_row.1, f32[1,128]{1,0:T(1,128)} %gain_row.1, s32[96]{0:T(128)} %slot_ids.1, ...), custom_call_target="tpu_custom_call" | custom-call | tf_op jit(solution)/shard_map/pallas_call | solution.py:507
  255.6 2.8 %copy.10 = bf16[1,1,576,1536]{3,2,1,0:T(8,128)(2,1)} copy(bf16[1,1,576,1536]{3,2,1,0:T(8,128)(2,1)} %shard_map.82) | data formatting | bytes 3538944
